TPU v7x, 256 devices: a whole 4x4x8 slice. The times are simulated.
256 devices in a mesh: chan: 64 (over x, z, core), tm: 4 (over y).
Axes of the slice: x: 4, y: 4, z: 8, core: 2. Of those that a mesh axis runs over, the one named last changes fastest.
Arguments:
- voltages: bfloat16 [2, 128, 512, 8192], P(None, 'chan', None, 'tm'), may hold values from -6 to 6
- weights: bfloat16 [2, 128, 512, 512], P(None, 'chan'), may hold values from -0.1875 to 0.1875
- baseline: float32 [128, 512], P(None, 'chan'), may hold values from 28 to 36
- gains: float32 [128, 512], P(None, 'chan'), may hold values from 0.02 to 0.2
- offsets: int32 [128], replicated, may hold values from 0 to 4, as said below
- shifts: int32 [4, 128], replicated, may hold values from 0 to 8, as said below
- delays: int32 [8, 8], replicated, may hold values from 0 to 12, as said below
Outputs:
- dedispersed: float32 [128, 512, 512], P(None, 'chan', 'tm')
Inputs may be any that keep to these rules, and one draw needn't show every extreme that they name: `offsets`: the largest value is reached in every draw. In section s the shifts are at most 2 ** s, and each section has a row at that bound. `delays`: the largest value is reached in every draw.
All inputs are finite; a program needn't handle non-finite values.
Results may differ from a plain program's by a relative error of at most 0.0011.
Values may be sent and summed in bfloat16 or wider, within the bound.
No kernel may reach another device: no remote copies, remote signals or barrier semaphores. Data moves between devices by JAX's collectives and lax.ppermute only.
A program may use at most 256 MiB of HBM per device.

v0:
```python
import jax
import jax.numpy as jnp
from jax import lax
from jax.sharding import PartitionSpec as P

BIN = 16
LEVELS = 4
OFFMAX = 4
TAIL = 31


def from_behind(value, axis, steps):
    count = lax.axis_size(axis)
    leading, last = (max(0, -steps), min(count, count - steps))
    return lax.ppermute(value, axis, [(source, source + steps) for source in range(leading, last)])


def dedisperse(series, offsets, shifts, delays, out_len):
    channels, beams_here, padded_len = series.shape
    start_len = padded_len - OFFMAX
    current = jax.vmap(
        lambda series_row, start_at: lax.dynamic_slice_in_dim(series_row, start_at, start_len, 1)
    )(series, offsets).astype(jnp.float32)
    for level_idx in range(LEVELS):
        half_size = 2**level_idx
        cur_len = current.shape[2]
        new_len = cur_len - half_size
        blocks = current.reshape(channels // (2 * half_size), 2, half_size, beams_here, cur_len)
        lower_rows = jnp.repeat(blocks[:, 0], 2, axis=1).reshape(channels, beams_here, cur_len)
        upper_rows = jnp.repeat(blocks[:, 1], 2, axis=1).reshape(channels, beams_here, cur_len)
        shifted = jax.vmap(
            lambda series_row, start_at: lax.dynamic_slice_in_dim(series_row, start_at, new_len, 1)
        )(upper_rows, shifts[level_idx])
        current = lower_rows[:, :, :new_len] + shifted
    tree_rows = 2**LEVELS
    grouped = current.reshape(channels // tree_rows, tree_rows, beams_here, current.shape[2])

    def coarse_trial(lag_row):
        aligned = jax.vmap(
            lambda group_block, start_at: lax.dynamic_slice_in_dim(
                group_block, start_at, out_len, 2
            )
        )(grouped, lag_row)
        return jnp.sum(aligned, axis=0)

    summed = lax.map(coarse_trial, delays)
    return summed.reshape(delays.shape[0] * tree_rows, beams_here, out_len)


def bin_time(detected):
    leading = detected.shape[:-1]
    return jnp.sum(detected.reshape(leading + (detected.shape[-1] // BIN, BIN)), axis=-1)


def late_extend(normalized):
    following = from_behind(normalized[:, :, :TAIL], "tm", -1)
    return jnp.concatenate([normalized, following], axis=2)


def per_device(voltages, weights, baseline, gains, offsets, shifts, delays):
    sign_flip = jnp.array([1.0, -1.0], jnp.bfloat16).reshape(2, 1, 1, 1)
    real_part = jnp.einsum(
        "pcbf,pcft->cbt", weights * sign_flip, voltages, preferred_element_type=jnp.float32
    )
    imag_part = jnp.einsum(
        "pcbf,pcft->cbt", weights[::-1], voltages, preferred_element_type=jnp.float32
    )
    detected = real_part * real_part + imag_part * imag_part
    window = voltages.shape[3] // BIN
    detected = bin_time(detected)
    regrouped = lax.all_to_all(detected, "chan", split_axis=1, concat_axis=0, tiled=True)
    normalized = ((regrouped - baseline[:, :, None]) * gains[:, :, None]).astype(jnp.bfloat16)
    extended = late_extend(normalized)
    return dedisperse(extended, offsets, shifts, delays, window)


def solution(mesh):
    placed = (
        P(None, "chan", None, "tm"),
        P(None, "chan", None, None),
        P(None, "chan"),
        P(None, "chan"),
        P(),
        P(),
        P(),
    )
    return jax.shard_map(
        per_device, mesh=mesh, in_specs=placed, out_specs=P(None, "chan", "tm"), check_vma=False
    )
```

profile of v0, /device:TPU:1, one launch (start us, length us, event | category | flops | bytes accessed | tf_op | source)
XLA Modules:
  0.0 422.6 jit_solution(6883892177572181484)
XLA Ops:
  0.0 1.7 rev.3
  1.7 7.8 %fusion.5 = f32[2,512,2048,1]{2,1,0,3:T(8,128)S(1)} fusion(bf16[2,2,512,2048]{3,2,1,0:T(8,128)(2,1)} %param.10, bf16[2,2,512,512]{3,2,1,0:T(8,128)(2,1)} %param.11, bf16[2]{0:T(256)(128)(2,1)} %constant.25.clone), kind=kOutput, calls=%fused_computation.26 | convolution fusion | flops 4296015872 | bytes 18874372 | tf_op jit(solution)/shard_map/pcbf,pcft->cbt/dot_general | solution.py:62
  9.5 6.9 %fusion.4 = f32[2,512,2048]{2,1,0:T(8,128)} fusion(f32[2,512,2048,1]{2,1,0,3:T(8,128)S(1)} %fusion.5, bf16[2,2,512,512]{3,2,1,0:T(8,128)(2,1)S(1)} %rev.3, bf16[2,2,512,2048]{3,2,1,0:T(8,128)(2,1)S(1)} %copy-done), kind=kOutput, calls=%fused_computation.18 | convolution fusion | flops 4301258752 | bytes 27262976 | tf_op jit(solution)/shard_map/pcbf,pcft->cbt/dot_general | solution.py:65
  16.4 8.7 %copy.53 = f32[2,512,2048]{1,2,0:T(8,128)} copy(f32[2,512,2048]{2,1,0:T(8,128)} %fusion.4) | data formatting | bytes 16777216 | tf_op jit(solution)/shard_map/add | solution.py:68
  25.1 5.4 %bitcast_reduce_fusion = f32[2,512,128]{1,2,0:T(8,128)S(1)} fusion(f32[2,512,2048]{1,2,0:T(8,128)} %copy.53), kind=kLoop, calls=%fused_computation.16 | loop fusion | flops 1966080 | bytes 8912896 | tf_op jit(solution)/shard_map/reduce_sum | solution.py:52
  30.5 1.0 copy.54
  31.5 13.0 %all-to-all-start = ((f32[2,512,128]{2,0,1:T(2,128)}), f32[2,512,128]{2,0,1:T(2,128)S(1)}, u32[]{:S(2)}, u32[]{:S(2)}) async-start(f32[2,512,128]{2,0,1:T(2,128)} %copy.54), calls=%async_computation | async-start | bytes 1048576 | tf_op jit(solution)/shard_map/all_to_all | solution.py:71
  44.7 17.1 %all-to-all-done = f32[2,512,128]{2,0,1:T(2,128)S(1)} async-done(((f32[2,512,128]{2,0,1:T(2,128)}), f32[2,512,128]{2,0,1:T(2,128)S(1)}, u32[]{:S(2)}, u32[]{:S(2)}) %all-to-all-start) | async-done | bytes 524320 | tf_op jit(solution)/shard_map/all_to_all | solution.py:71
  62.5 1.8 collective-permute-start
  64.2 3.2 collective-permute-done
  67.8 9.8 %copy.61 = bf16[128,8,159]{1,0,2:T(8,128)(2,1)} copy(bf16[128,8,159]{2,1,0:T(8,128)(2,1)S(1)} %pad_maximum_fusion) | data formatting | bytes 651264 | tf_op jit(solution)/shard_map/concatenate | solution.py:57
  77.6 20.5 %gather_fusion.1 = bf16[128,8,155]{1,0,2:T(8,128)(2,1)} fusion(bf16[128,8,159]{1,0,2:T(8,128)(2,1)} %copy.61, s32[128]{0:T(128)S(1)} %fusion.30), kind=kCustom, calls=%fused_computation.1 | custom fusion | bytes 636416 | tf_op jit(solution)/shard_map/vmap()/gather | solution.py:22
  98.1 12.4 %fusion.31 = (f32[64,1,1,8,155]{3,1,0,4,2:T(1,128)}, f32[64,1,1,8,155]{3,1,0,4,2:T(1,128)S(1)}) fusion(bf16[64,2,1,8,155]{3,1,0,4,2:T(2,128)(2,1)} %bitcast.112), kind=kLoop, calls=%fused_computation.61 | loop fusion | bytes 1269760 | tf_op jit(solution)/shard_map/slice | solution.py:29
  110.5 5.5 %broadcast_in_dim.44 = f32[64,1,2,8,155]{3,2,0,4,1:T(2,128)} broadcast(f32[64,8,155]{1,0,2:T(8,128)S(1)} %bitcast.114), dimensions={0,3,4} | broadcast | bytes 952320 | tf_op jit(solution)/shard_map/broadcast_in_dim | solution.py:30
  116.0 21.2 %gather_fusion.2 = f32[128,8,154]{1,0,2:T(8,128)} fusion(f32[128,8,155]{1,0,2:T(8,128)} %bitcast.108, s32[128]{0:T(128)S(1)} %get-tuple-element.70), kind=kCustom, calls=%fused_computation.2 | custom fusion | bytes 1263104 | tf_op jit(solution)/shard_map/vmap()/gather | solution.py:32
  137.3 8.2 %broadcast_in_dim.43 = f32[64,1,2,8,155]{3,2,0,4,1:T(2,128)} broadcast(f32[64,8,155]{1,0,2:T(8,128)} %bitcast.113), dimensions={0,3,4} | broadcast | bytes 952320 | tf_op jit(solution)/shard_map/broadcast_in_dim | solution.py:29
  145.5 14.0 %slice_add_fusion = f32[128,8,154]{1,0,2:T(8,128)} fusion(f32[128,8,154]{1,0,2:T(8,128)} %gather_fusion.2, f32[128,8,155]{1,0,2:T(8,128)} %bitcast.100), kind=kLoop, calls=%fused_computation.12 | loop fusion | flops 157696 | bytes 1892352 | tf_op jit(solution)/shard_map/add | solution.py:34
  159.5 16.9 %slice_bitcast_fusion.1 = (f32[32,2,8,154]{2,1,0,3:T(2,128)}, f32[32,2,8,154]{2,1,0,3:T(2,128)}) fusion(f32[32,2,2,8,154]{3,2,1,0,4:T(2,128)} %bitcast.101), kind=kLoop, calls=%fused_computation.21 | loop fusion | bytes 1261568 | tf_op jit(solution)/shard_map/squeeze | solution.py:29
  176.4 8.4 %broadcast_in_dim.46 = f32[32,2,2,8,154]{3,2,1,0,4:T(2,128)} broadcast(f32[32,2,8,154]{2,1,0,3:T(2,128)} %get-tuple-element.61), dimensions={0,1,3,4} | broadcast | bytes 946176 | tf_op jit(solution)/shard_map/broadcast_in_dim | solution.py:30
  184.8 20.9 %gather_fusion.3 = f32[128,8,152]{1,0,2:T(8,128)} fusion(f32[128,8,154]{1,0,2:T(8,128)} %bitcast.109, s32[128]{0:T(128)S(1)} %get-tuple-element.69), kind=kCustom, calls=%fused_computation.3 | custom fusion | bytes 1246720 | tf_op jit(solution)/shard_map/vmap()/gather | solution.py:32
  205.8 8.0 %broadcast_in_dim.45 = f32[32,2,2,8,154]{3,2,1,0,4:T(2,128)} broadcast(f32[32,2,8,154]{2,1,0,3:T(2,128)} %get-tuple-element.60), dimensions={0,1,3,4} | broadcast | bytes 946176 | tf_op jit(solution)/shard_map/broadcast_in_dim | solution.py:29
  213.7 13.8 %slice_add_fusion.1 = f32[128,8,152]{1,0,2:T(8,128)} fusion(f32[128,8,152]{1,0,2:T(8,128)} %gather_fusion.3, f32[128,8,154]{1,0,2:T(8,128)} %bitcast.102), kind=kLoop, calls=%fused_computation.13 | loop fusion | flops 155648 | bytes 1867776 | tf_op jit(solution)/shard_map/add | solution.py:34
  227.5 9.6 %slice_bitcast_fusion.3 = (f32[16,4,8,152]{2,1,0,3:T(4,128)}, f32[16,4,8,152]{2,1,0,3:T(4,128)S(1)}) fusion(f32[16,2,4,8,152]{3,2,1,0,4:T(4,128)} %bitcast.103), kind=kLoop, calls=%fused_computation.23 | loop fusion | bytes 1245184 | tf_op jit(solution)/shard_map/squeeze | solution.py:29
  237.2 5.5 %broadcast_in_dim.48 = f32[16,4,2,8,152]{3,2,1,0,4:T(2,128)} broadcast(f32[16,4,8,152]{2,1,0,3:T(4,128)S(1)} %get-tuple-element.63), dimensions={0,1,3,4} | broadcast | bytes 933888 | tf_op jit(solution)/shard_map/broadcast_in_dim | solution.py:30
  242.7 20.5 %gather_fusion.4 = f32[128,8,148]{1,0,2:T(8,128)} fusion(f32[128,8,152]{1,0,2:T(8,128)} %bitcast.110, s32[128]{0:T(128)S(1)} %get-tuple-element.71), kind=kCustom, calls=%fused_computation.4 | custom fusion | bytes 1213952 | tf_op jit(solution)/shard_map/vmap()/gather | solution.py:32
  263.2 7.9 %broadcast_in_dim.47 = f32[16,4,2,8,152]{3,2,1,0,4:T(2,128)} broadcast(f32[16,4,8,152]{2,1,0,3:T(4,128)} %get-tuple-element.62), dimensions={0,1,3,4} | broadcast | bytes 933888 | tf_op jit(solution)/shard_map/broadcast_in_dim | solution.py:29
  271.1 13.5 %slice_add_fusion.2 = f32[128,8,148]{1,0,2:T(8,128)} fusion(f32[128,8,148]{1,0,2:T(8,128)} %gather_fusion.4, f32[128,8,152]{1,0,2:T(8,128)} %bitcast.104), kind=kLoop, calls=%fused_computation.14 | loop fusion | flops 151552 | bytes 1818624 | tf_op jit(solution)/shard_map/add | solution.py:34
  284.7 7.5 %slice_bitcast_fusion.5 = (f32[8,8,8,148]{2,1,0,3:T(8,128)}, f32[8,8,8,148]{2,1,0,3:T(8,128)S(1)}) fusion(f32[8,2,8,8,148]{3,2,1,0,4:T(8,128)} %bitcast.105), kind=kLoop, calls=%fused_computation.25 | loop fusion | bytes 1212416 | tf_op jit(solution)/shard_map/squeeze | solution.py:29
  292.1 5.5 %broadcast_in_dim.50 = f32[8,8,2,8,148]{3,2,1,0,4:T(2,128)} broadcast(f32[8,8,8,148]{2,1,0,3:T(8,128)S(1)} %get-tuple-element.65), dimensions={0,1,3,4} | broadcast | bytes 909312 | tf_op jit(solution)/shard_map/broadcast_in_dim | solution.py:30
  297.7 19.5 %gather_fusion.5 = f32[128,8,140]{1,0,2:T(8,128)} fusion(f32[128,8,148]{1,0,2:T(8,128)} %bitcast.111, s32[128]{0:T(128)S(1)} %get-tuple-element.68), kind=kCustom, calls=%fused_computation.5 | custom fusion | bytes 1148416 | tf_op jit(solution)/shard_map/vmap()/gather | solution.py:32
  317.2 7.7 %broadcast_in_dim.49 = f32[8,8,2,8,148]{3,2,1,0,4:T(2,128)} broadcast(f32[8,8,8,148]{2,1,0,3:T(8,128)} %get-tuple-element.64), dimensions={0,1,3,4} | broadcast | bytes 909312 | tf_op jit(solution)/shard_map/broadcast_in_dim | solution.py:29
  324.9 12.9 %slice_add_fusion.3 = f32[128,8,140]{1,0,2:T(8,128)} fusion(f32[128,8,140]{1,0,2:T(8,128)} %gather_fusion.5, f32[128,8,148]{1,0,2:T(8,128)} %bitcast.106), kind=kLoop, calls=%fused_computation.15 | loop fusion | flops 143360 | bytes 1720320 | tf_op jit(solution)/shard_map/add | solution.py:34
  337.8 8.4 %copy.62 = f32[8,16,8,140]{1,2,0,3:T(8,128)} copy(f32[8,16,8,140]{2,1,0,3:T(8,128)} %bitcast.107) | data formatting | bytes 1146880 | tf_op jit(solution)/shard_map/while | solution.py:46
  346.1 76.3 %while.10 = (s32[]{:T(128)}, f32[8,16,8,128]{3,2,1,0:T(8,128)}, s32[8,8]{1,0:T(8,128)}, f32[8,16,8,140]{1,2,0,3:T(8,128)}, s32[]{:T(128)}, /*index=5*/f32[]{:T(128)}) while((s32[]{:T(128)}, f32[8,16,8,128]{3,2,1,0:T(8,128)}, s32[8,8]{1,0:T(8,128)}, f32[8,16,8,140]{1,2,0,3:T(8,128)}, s32[]{:T(128)}, /*index=5*/f32[]{:T(128)}) %tuple.31), condition=%wide.region_3.4_spmd, body=%wide.region_1.3_spmd.sunk | while | flops 114754 | bytes 1901325 | solution.py:46
  346.1 0.7 fusion.36
  346.8 5.5 %gather_fusion = f32[8,16,8,128]{1,2,3,0:T(8,128)} fusion(f32[8,16,8,140]{1,2,0,3:T(8,128)} %get-tuple-element.112, s32[8]{0:T(128)S(1)} %fusion.36), kind=kCustom, calls=%fused_computation.clone.1 | custom fusion | bytes 1048704 | tf_op jit(solution)/shard_map/while/body/eval_jaxpr/vmap()/gather | solution.py:40
  352.3 2.5 reduce_sum.21
  355.0 0.7 constant_dynamic-update-slice_fusion.2
  355.7 0.7 fusion.36
  356.4 5.5 %gather_fusion = f32[8,16,8,128]{1,2,3,0:T(8,128)} fusion(f32[8,16,8,140]{1,2,0,3:T(8,128)} %get-tuple-element.112, s32[8]{0:T(128)S(1)} %fusion.36), kind=kCustom, calls=%fused_computation.clone.1 | custom fusion | bytes 1048704 | tf_op jit(solution)/shard_map/while/body/eval_jaxpr/vmap()/gather | solution.py:40
  361.8 2.5 reduce_sum.21
  364.5 0.7 constant_dynamic-update-slice_fusion.2
  365.2 0.7 fusion.36
  365.9 5.5 %gather_fusion = f32[8,16,8,128]{1,2,3,0:T(8,128)} fusion(f32[8,16,8,140]{1,2,0,3:T(8,128)} %get-tuple-element.112, s32[8]{0:T(128)S(1)} %fusion.36), kind=kCustom, calls=%fused_computation.clone.1 | custom fusion | bytes 1048704 | tf_op jit(solution)/shard_map/while/body/eval_jaxpr/vmap()/gather | solution.py:40
  371.4 2.5 reduce_sum.21
  374.1 0.7 constant_dynamic-update-slice_fusion.2
  374.7 0.7 fusion.36
  375.4 5.5 %gather_fusion = f32[8,16,8,128]{1,2,3,0:T(8,128)} fusion(f32[8,16,8,140]{1,2,0,3:T(8,128)} %get-tuple-element.112, s32[8]{0:T(128)S(1)} %fusion.36), kind=kCustom, calls=%fused_computation.clone.1 | custom fusion | bytes 1048704 | tf_op jit(solution)/shard_map/while/body/eval_jaxpr/vmap()/gather | solution.py:40
  380.9 2.5 reduce_sum.21
  383.6 0.7 constant_dynamic-update-slice_fusion.2
  384.3 0.7 fusion.36
  385.0 5.5 %gather_fusion = f32[8,16,8,128]{1,2,3,0:T(8,128)} fusion(f32[8,16,8,140]{1,2,0,3:T(8,128)} %get-tuple-element.112, s32[8]{0:T(128)S(1)} %fusion.36), kind=kCustom, calls=%fused_computation.clone.1 | custom fusion | bytes 1048704 | tf_op jit(solution)/shard_map/while/body/eval_jaxpr/vmap()/gather | solution.py:40
  390.4 2.5 reduce_sum.21
  393.8 0.7 fusion.36
  394.5 5.5 %gather_fusion = f32[8,16,8,128]{1,2,3,0:T(8,128)} fusion(f32[8,16,8,140]{1,2,0,3:T(8,128)} %get-tuple-element.112, s32[8]{0:T(128)S(1)} %fusion.36), kind=kCustom, calls=%fused_computation.clone.1 | custom fusion | bytes 1048704 | tf_op jit(solution)/shard_map/while/body/eval_jaxpr/vmap()/gather | solution.py:40
  400.0 2.5 reduce_sum.21
  403.3 0.7 fusion.36
  404.0 5.5 %gather_fusion = f32[8,16,8,128]{1,2,3,0:T(8,128)} fusion(f32[8,16,8,140]{1,2,0,3:T(8,128)} %get-tuple-element.112, s32[8]{0:T(128)S(1)} %fusion.36), kind=kCustom, calls=%fused_computation.clone.1 | custom fusion | bytes 1048704 | tf_op jit(solution)/shard_map/while/body/eval_jaxpr/vmap()/gather | solution.py:40
  409.5 2.5 reduce_sum.21
  412.2 0.7 constant_dynamic-update-slice_fusion.2
  412.9 0.7 fusion.36
  413.6 5.5 %gather_fusion = f32[8,16,8,128]{1,2,3,0:T(8,128)} fusion(f32[8,16,8,140]{1,2,0,3:T(8,128)} %get-tuple-element.112, s32[8]{0:T(128)S(1)} %fusion.36), kind=kCustom, calls=%fused_computation.clone.1 | custom fusion | bytes 1048704 | tf_op jit(solution)/shard_map/while/body/eval_jaxpr/vmap()/gather | solution.py:40
  419.0 2.5 reduce_sum.21
  421.7 0.7 constant_dynamic-update-slice_fusion.2
  (31 shorter events, 4.1 us)
Async XLA Ops:
  1.7 7.8 %copy-start = (bf16[2,2,512,2048]{3,2,1,0:T(8,128)(2,1)S(1)}, bf16[2,2,512,2048]{3,2,1,0:T(8,128)(2,1)}, u32[]{:S(2)}) copy-start(bf16[2,2,512,2048]{3,2,1,0:T(8,128)(2,1)} %param.10) | copy-start | bytes 25165828
  25.1 19.4 %copy-start.1 = (f32[128,8]{0,1:T(8,128)S(1)}, f32[128,8]{0,1:T(8,128)}, u32[]{:S(2)}) copy-start(f32[128,8]{0,1:T(8,128)} %param.12) | copy-start | bytes 12292
  25.1 19.5 %copy-start.2 = (f32[128,8]{0,1:T(8,128)S(1)}, f32[128,8]{0,1:T(8,128)}, u32[]{:S(2)}) copy-start(f32[128,8]{0,1:T(8,128)} %param.13) | copy-start | bytes 12292
  25.1 19.6 %copy-start.3 = (s32[4,128]{1,0:T(4,128)S(1)}, s32[4,128]{1,0:T(4,128)}, u32[]{:S(2)}) copy-start(s32[4,128]{1,0:T(4,128)} %param.15) | copy-start | bytes 6148
  25.1 39.1 %copy-start.4 = (s32[128]{0:T(128)S(1)}, s32[128]{0:T(128)}, u32[]{:S(2)}) copy-start(s32[128]{0:T(128)} %param.14) | copy-start | bytes 1540
  31.5 30.3 %all-to-all-start = ((f32[2,512,128]{2,0,1:T(2,128)}), f32[2,512,128]{2,0,1:T(2,128)S(1)}, u32[]{:S(2)}, u32[]{:S(2)}) async-start(f32[2,512,128]{2,0,1:T(2,128)} %copy.54), calls=%async_computation | async-start | bytes 1048576 | tf_op jit(solution)/shard_map/all_to_all | solution.py:71
  62.5 5.0 %collective-permute-start = (bf16[128,8,31]{0,1,2:T(8,128)(2,1)S(1)}, bf16[128,8,31]{0,1,2:T(8,128)(2,1)S(1)}, u32[]{:S(2)}, u32[]{:S(2)}) collective-permute-start(bf16[128,8,31]{0,1,2:T(8,128)(2,1)S(1)} %copy.59), channel_id=1, source_target_pairs={{1,0},{2,1},{3,2},{5,4},{6,5},{7,6},{9,8},{10,9},{11,10},{13,12},{... | collective-permute-start | bytes 190472 | tf_op jit(solution)/shard_map/ppermute | solution.py:15
where the time goes:
time: 430 us; the launch traced here: 423 us
  local copies, waits for them, and re-layouts  287 us (67%)
  other arithmetic  85.8 us (20%)
  waiting for transfers between devices  20.3 us (5%)
  matrix products  14.7 us (3%)
  starting transfers between devices  14.7 us (3%)
    gather x4, local copies, waits for them, and re-layouts, dedisperse(): lax.dynamic_slice_in_dim(series_row, start_at, new_len, 1)  82.2 us
    add x4, other arithmetic, dedisperse(): current = lower_rows[:, :, :new_len] + shifted  54.2 us
    gather x8, local copies, waits for them, and re-layouts, coarse_trial(): lax.dynamic_slice_in_dim(group_block, start_at, out_len, 2)  43.7 us
    squeeze x3, local copies, waits for them, and re-layouts, dedisperse(): blocks[:, 0]  34.1 us
    broadcast_in_dim x4, local copies, waits for them, and re-layouts, dedisperse(): jnp.repeat(blocks[:, 0], 2, axis=1).reshape(channels, beams_here, cur_len)  31.8 us
    broadcast_in_dim x4, local copies, waits for them, and re-layouts, dedisperse(): jnp.repeat(blocks[:, 1], 2, axis=1).reshape(channels, beams_here, cur_len)  25 us
    gather x1, local copies, waits for them, and re-layouts, dedisperse(): lax.dynamic_slice_in_dim(series_row, start_at, start_len, 1)  20.5 us
    reduce_sum x8, other arithmetic, coarse_trial(): return jnp.sum(aligned, axis=0)  20.2 us
  transfers between devices with their start and end apart: 2, of which 2 were waited for; matrix products, arithmetic and copies ran while one was open for 0% of the time, Pallas kernels for 0%

commit v1 on v0

v1 whole, which is shorter than its diff:
```python
import functools
import jax
import jax.numpy as jnp
from jax import lax
from jax.experimental import pallas as pl
from jax.experimental.pallas import tpu as pltpu
from jax.sharding import PartitionSpec as P

LANES = 128
F32 = jnp.float32
BF16 = jnp.bfloat16
BIN = 16


def roll_lanes(x, steps):
    return pltpu.roll(x, steps % LANES, 1)


def fold_pair(a, b, stride):
    lane = lax.broadcasted_iota(jnp.int32, a.shape, 1)
    upper = (lane & stride) != 0
    return jnp.where(upper, b + roll_lanes(b, stride), a + roll_lanes(a, -stride))


def fold(tiles, stride):
    while len(tiles) > 1:
        tiles = [fold_pair(tiles[i], tiles[i + 1], stride) for i in range(0, len(tiles), 2)]
        stride *= 2
    return tiles[0]


def beamform_kernel(rows, v_ref, w_ref, out_ref, stacked, part, binned):
    channel, step = pl.program_id(0), pl.program_id(1)
    steps = pl.num_programs(1)
    beams, feeds = w_ref.shape[2:]
    width = v_ref.shape[3]

    @pl.when(step == 0)
    def _():
        for r in range(beams // rows):
            lo = 2 * r * rows
            src = pl.ds(r * rows, rows)
            stacked[lo : lo + rows, :feeds] = w_ref[0, 0, src, :]
            stacked[lo : lo + rows, feeds:] = -w_ref[1, 0, src, :]
            stacked[lo + rows : lo + 2 * rows, :feeds] = w_ref[1, 0, src, :]
            stacked[lo + rows : lo + 2 * rows, feeds:] = w_ref[0, 0, src, :]

    volts = v_ref[...].reshape(2 * feeds, width)
    for r in range(beams // rows):
        lo = 2 * r * rows
        both = jnp.dot(stacked[lo : lo + 2 * rows, :], volts, preferred_element_type=F32)
        real, imag = both[:rows], both[rows:]
        power = real * real + imag * imag
        tiles = [power[:, i : i + LANES] for i in range(0, width, LANES)]
        part[step, r * rows : (r + 1) * rows, :] = fold(tiles, 1)

    @pl.when(step == steps - 1)
    def _():
        count = 4
        stride = width // LANES
        total = fold([part[i] for i in range(count)], stride)
        lane = lax.broadcasted_iota(jnp.int32, total.shape, 1)
        source = ((lane & 7) << 4) | (lane >> 3)
        total = jnp.take_along_axis(total, source, axis=1)
        out_ref[:, pl.ds(pl.multiple_of(channel * 8, 8), 8), :] = total.reshape(beams // 8, 8, LANES)


def beamform(voltages, weights, rows=256, width=512):
    _, channels, feeds, samples = voltages.shape
    beams = weights.shape[2]
    steps = samples // width
    return pl.pallas_call(
        functools.partial(beamform_kernel, rows),
        grid=(channels, steps),
        in_specs=[
            pl.BlockSpec((2, 1, feeds, width), lambda c, i: (0, c, 0, i)),
            pl.BlockSpec((2, 1, beams, feeds), lambda c, i: (0, c, 0, 0)),
        ],
        out_specs=pl.BlockSpec((beams // 8, 8 * channels, LANES), lambda c, i: (0, 0, 0)),
        out_shape=jax.ShapeDtypeStruct((beams // 8, 8 * channels, LANES), F32),
        scratch_shapes=[
            pltpu.VMEM((2 * beams, 2 * feeds), BF16),
            pltpu.VMEM((steps, beams, LANES), F32),
            pltpu.VMEM((8, LANES), F32),
        ],
        compiler_params=pltpu.CompilerParams(
            dimension_semantics=("arbitrary", "arbitrary"), vmem_limit_bytes=48 * 1024 * 1024
        ),
    )(voltages, weights)


LEVELS = 4
TREE = 16
TAPS = 32
VMEM = 48 * 1024 * 1024


def taps_kernel(offsets_ref, shifts_ref, delays_ref, taps_ref):
    rows = lax.broadcasted_iota(jnp.int32, (LANES, LANES), 0)
    cols = lax.broadcasted_iota(jnp.int32, (LANES, LANES), 1)
    tree_row = rows & (TREE - 1)
    delay = jnp.broadcast_to(offsets_ref[...], (LANES, LANES)).astype(F32)
    for level in range(LEVELS):
        half = 2**level
        block = 2 * half
        here = (cols & (block - 1)) == (tree_row >> (LEVELS - 1 - level))
        held = jnp.where(here, shifts_ref[level : level + 1, :], 0).astype(F32).astype(BF16)
        reach = ((rows >> (level + 1)) == (cols >> (level + 1))) & ((cols & half) != 0)
        delay += jnp.dot(held, jnp.where(reach, 1.0, 0.0).astype(BF16), preferred_element_type=F32)
    groups = delays_ref.shape[1]
    row8 = lax.broadcasted_iota(jnp.int32, (groups, LANES), 0)
    col8 = lax.broadcasted_iota(jnp.int32, (groups, LANES), 1)
    of_group = jnp.where(row8 == (col8 >> LEVELS), 1.0, 0.0).astype(BF16)
    spread = jnp.dot(
        delays_ref[...].astype(F32).astype(BF16), of_group, preferred_element_type=F32
    )
    delay = delay.reshape(groups, TREE, LANES) + spread.reshape(groups, 1, LANES)
    delay = delay.reshape(LANES, LANES).astype(jnp.int32)
    for d in range(TAPS):
        taps_ref[:, d * LANES : (d + 1) * LANES] = jnp.where(delay == d, 1.0, 0.0).astype(BF16)


def make_taps(offsets, shifts, delays):
    return pl.pallas_call(
        taps_kernel,
        out_shape=jax.ShapeDtypeStruct((LANES, TAPS * LANES), BF16),
        cost_estimate=pl.CostEstimate(flops=4_000_000, bytes_accessed=1_100_000, transcendentals=0),
    )(offsets.reshape(1, LANES), shifts, delays)


def normalize(x, baseline_ref, gains_ref, b):
    return ((x - baseline_ref[:, b : b + 1]) * gains_ref[:, b : b + 1]).astype(BF16)


def own_kernel(taps_ref, binned_ref, baseline_ref, gains_ref, out_ref, *windows):
    beams = baseline_ref.shape[1]
    lane = lax.broadcasted_iota(jnp.int32, (LANES, LANES), 1)
    for pair in range(beams // 2):
        window = windows[pair % len(windows)]
        for j in range(2):
            b = 2 * pair + j
            x = normalize(binned_ref[pl.ds(b, LANES, stride=beams), :], baseline_ref, gains_ref, b)
            x = x.astype(F32)
            for d in range(TAPS):
                moved = x if d == 0 else jnp.where(lane < LANES - d, pltpu.roll(x, LANES - d, 1), 0.0)
                window[d * LANES : (d + 1) * LANES, j * LANES : (j + 1) * LANES] = moved.astype(BF16)
        both = jnp.dot(taps_ref[...], window[...], preferred_element_type=F32)
        for j in range(2):
            out_ref[pl.ds(2 * pair + j, LANES, stride=beams), :] = both[:, j * LANES : (j + 1) * LANES]


def dedisperse_own(taps, binned, baseline, gains):
    beams = baseline.shape[1]
    return pl.pallas_call(
        own_kernel,
        out_shape=jax.ShapeDtypeStruct((LANES * beams, LANES), F32),
        scratch_shapes=[pltpu.VMEM((TAPS * LANES, 2 * LANES), BF16)] * 2,
        compiler_params=pltpu.CompilerParams(vmem_limit_bytes=VMEM),
        cost_estimate=pl.CostEstimate(flops=4_000_000_000, bytes_accessed=3_000_000, transcendentals=0),
    )(taps, binned, baseline, gains)


def tail_kernel(taps_ref, tail_ref, baseline_ref, gains_ref, own_ref, out_ref, window):
    beams = baseline_ref.shape[1]
    per = LANES // TAPS
    lane = lax.broadcasted_iota(jnp.int32, (LANES, LANES), 1)
    for j in range(beams // per):
        x = jnp.concatenate(
            [
                normalize(tail_ref[pl.ds(b, LANES, stride=beams), :], baseline_ref, gains_ref, b).astype(F32)
                for b in range(j * per, (j + 1) * per)
            ],
            axis=1,
        )
        for d in range(TAPS):
            keep = (lane & (TAPS - 1)) >= TAPS - d
            moved = jnp.where(keep, pltpu.roll(x, (TAPS - d) % LANES, 1), 0.0)
            window[d * LANES : (d + 1) * LANES, j * LANES : (j + 1) * LANES] = moved.astype(BF16)
    added = jnp.dot(taps_ref[...], window[...], preferred_element_type=F32)
    for b in range(beams):
        rows = pl.ds(b, LANES, stride=beams)
        own = own_ref[rows, :]
        piece = added[:, b * TAPS : (b + 1) * TAPS]
        full = jnp.concatenate([jnp.zeros((LANES, LANES - TAPS), F32), piece], axis=1)
        out_ref[rows, :] = own + full


def add_tail(taps, tail, baseline, gains, own):
    beams = baseline.shape[1]
    return pl.pallas_call(
        tail_kernel,
        out_shape=jax.ShapeDtypeStruct((LANES * beams, LANES), F32),
        scratch_shapes=[pltpu.VMEM((TAPS * LANES, 2 * LANES), BF16)],
        compiler_params=pltpu.CompilerParams(vmem_limit_bytes=VMEM),
        input_output_aliases={4: 0},
        cost_estimate=pl.CostEstimate(flops=1_000_000_000, bytes_accessed=2_000_000, transcendentals=0),
    )(taps, tail, baseline, gains, own)


def from_behind(value, axis):
    count = lax.axis_size(axis)
    return lax.ppermute(value, axis, [(source, source - 1) for source in range(1, count)])


def per_device(voltages, weights, baseline, gains, offsets, shifts, delays):
    binned = beamform(voltages, weights)
    regrouped = lax.all_to_all(binned, "chan", split_axis=0, concat_axis=0, tiled=True)
    taps = make_taps(offsets, shifts, delays)
    channels, beams = baseline.shape
    regrouped = regrouped.reshape(channels * beams, LANES)
    following = from_behind(regrouped[:, :TAPS], "tm")
    inside = (lax.axis_index("tm") < lax.axis_size("tm") - 1).astype(F32)
    own = dedisperse_own(taps, regrouped, baseline, gains)
    full = add_tail(taps, following, baseline, gains * inside, own)
    return full.reshape(channels, beams, LANES)


def solution(mesh):
    placed = (
        P(None, "chan", None, "tm"),
        P(None, "chan", None, None),
        P(None, "chan"),
        P(None, "chan"),
        P(),
        P(),
        P(),
    )
    return jax.shard_map(
        per_device, mesh=mesh, in_specs=placed, out_specs=P(None, "chan", "tm"), check_vma=False
    )
```

time: 430 us -> 66.1 us (0.15); the launches traced: 423 us -> 65.8 us
  local copies, waits for them, and re-layouts: 287 us -> 3.02 us
  other arithmetic: 85.8 us -> 0.01 us
  Pallas kernels: 0 us -> 25.2 us
  matrix products: 14.7 us -> 0 us
    gather x13 -> x0, local copies, waits for them, and re-layouts: 146 us -> none  [the longest x4 82.2 us: dedisperse(): lax.dynamic_slice_in_dim(series_row, start_at, new_len, 1)]
    broadcast_in_dim x8 -> x0, local copies, waits for them, and re-layouts: 56.7 us -> none  [the longest x4 31.8 us: dedisperse(): jnp.repeat(blocks[:, 0], 2, axis=1).reshape(channels, beams_here, cur_len)]
    add x4 -> x0, other arithmetic: 54.2 us -> none  [dedisperse(): current = lower_rows[:, :, :new_len] + shifted]
    squeeze x3 -> x0, local copies, waits for them, and re-layouts: 34.1 us -> none  [dedisperse(): blocks[:, 0]]
    reduce_sum x9 -> x0, other arithmetic: 25.5 us -> none  [the longest x8 20.2 us: coarse_trial(): return jnp.sum(aligned, axis=0)]
    pallas_call x0 -> x4, Pallas kernels: none -> 25.2 us  [the longest x1 15.4 us: beamform(): pl.pallas_call(functools.partial(beamform_kernel, rows), grid=(channels,...]
    dot_general x2 -> x0, matrix products: 14.7 us -> none  [the longest x1 7.76 us: per_device(): jnp.einsum('pcbf,pcft->cbt', weights * sign_flip, voltages, preferred_ele...]
    slice x2 -> x0, local copies, waits for them, and re-layouts: 12.6 us -> none  [the longest x1 12.4 us: dedisperse(): blocks[:, 0]]
  transfers between devices with their start and end apart: 2 -> 2, of which waited for: 2 -> 2; matrix products, arithmetic and copies ran while one was open for 0% -> 0% of each run, Pallas kernels for 0% -> 10%
where the time goes in v1:
time: 66.1 us; the launch traced here: 65.8 us
  Pallas kernels  25.2 us (38%)
  waiting for transfers between devices  23.3 us (35%)
  starting transfers between devices  14.3 us (22%)
  local copies, waits for them, and re-layouts  3.02 us (5%)
    pallas_call x1, Pallas kernels, beamform(): pl.pallas_call(functools.partial(beamform_kernel, rows), grid=(channels,...  15.4 us
    all_to_all x1, waiting for transfers between devices, per_device(): lax.all_to_all(binned, 'chan', split_axis=0, concat_axis=0, tiled=True)  14.9 us
    all_to_all x1, starting transfers between devices, per_device(): lax.all_to_all(binned, 'chan', split_axis=0, concat_axis=0, tiled=True)  13 us
    ppermute x1, waiting for transfers between devices, from_behind(): lax.ppermute(value, axis, [(source, source - 1) for source in range(1, co...  8.37 us
    pallas_call x1, Pallas kernels, dedisperse_own(): pl.pallas_call(own_kernel, out_shape=jax.ShapeDtypeStruct((LANES * beams,...  4.19 us
    pallas_call x1, Pallas kernels, add_tail(): pl.pallas_call(tail_kernel, out_shape=jax.ShapeDtypeStruct((LANES * beams...  3.43 us
    unnamed x10, local copies, waits for them, and re-layouts  3.02 us
    pallas_call x1, Pallas kernels, make_taps(): pl.pallas_call(taps_kernel, out_shape=jax.ShapeDtypeStruct((LANES, TAPS *...  2.21 us
  transfers between devices with their start and end apart: 2, of which 2 were waited for; matrix products, arithmetic and copies ran while one was open for 0% of the time, Pallas kernels for 10%

profile of v1, /device:TPU:1, one launch (start us, length us, event | category | flops | bytes accessed | tf_op | source)
XLA Modules:
  0.0 65.8 jit_solution(14482858166439927146)
XLA Ops:
  0.0 0.0 copy-start
  0.0 1.6 %copy-done = bf16[2,2,512,512]{3,2,1,0:T(8,128)(2,1)S(1)} copy-done((bf16[2,2,512,512]{3,2,1,0:T(8,128)(2,1)S(1)}, bf16[2,2,512,512]{3,2,1,0:T(8,128)(2,1)}, u32[]{:S(2)}) %copy-start) | copy-done | bytes 2097176
  1.6 0.0 copy-start.2
  1.6 0.0 copy-start.3
  1.6 15.4 %shard_map.74 = f32[64,16,128]{2,1,0:T(8,128)} custom-call(bf16[2,2,512,2048]{3,2,1,0:T(8,128)(2,1)} %v_ref.1, bf16[2,2,512,512]{3,2,1,0:T(8,128)(2,1)S(1)} %copy-done), custom_call_target="tpu_custom_call" | custom-call | tf_op jit(solution)/shard_map/pallas_call | solution.py:72
  17.0 13.0 %all-to-all-start = ((f32[64,16,128]{2,1,0:T(8,128)}), f32[64,16,128]{2,1,0:T(8,128)S(1)}, u32[]{:S(2)}, u32[]{:S(2)}) async-start(f32[64,16,128]{2,1,0:T(8,128)} %shard_map.74), calls=%async_computation | async-start | bytes 1048576 | tf_op jit(solution)/shard_map/all_to_all | solution.py:207
  30.0 0.0 copy-done.2
  30.0 0.1 copy.13.gains_ref
  30.1 0.0 copy-done.3
  30.1 0.1 copy.17.baseline_ref
  30.2 2.2 %shard_map.73.taps_ref = bf16[128,4096]{1,0:T(8,128)(2,1)} custom-call(s32[1,128]{1,0:T(1,128)} %bitcast.6, s32[4,128]{1,0:T(4,128)} %shifts_ref.1, s32[8,8]{1,0:T(8,128)} %delays_ref.1), custom_call_target="tpu_custom_call" | custom-call | flops 4000000 | bytes 1100000 | tf_op jit(solution)/shard_map/pallas_call | solution.py:124
  32.4 14.9 %all-to-all-done = f32[64,16,128]{2,1,0:T(8,128)S(1)} async-done(((f32[64,16,128]{2,1,0:T(8,128)}), f32[64,16,128]{2,1,0:T(8,128)S(1)}, u32[]{:S(2)}, u32[]{:S(2)}) %all-to-all-start) | async-done | bytes 524320 | tf_op jit(solution)/shard_map/all_to_all | solution.py:207
  47.3 1.3 %collective-permute-start = (f32[1024,32]{1,0:T(8,128)S(1)}, f32[1024,32]{1,0:T(8,128)S(1)}, u32[]{:S(2)}, u32[]{:S(2)}) collective-permute-start(f32[1024,32]{1,0:T(8,128)S(1)} %bitcast.4), channel_id=1, source_target_pairs={{1,0},{2,1},{3,2},{5,4},{6,5},{7,6},{9,8},{10,9},{11,10},{13,12},{... | collective-permute-start | bytes 393224 | tf_op jit(solution)/shard_map/ppermute | solution.py:202
  48.6 0.0 copy-start.1
  48.6 1.2 %copy-done.1 = bf16[128,4096]{1,0:T(8,128)(2,1)S(1)} copy-done((bf16[128,4096]{1,0:T(8,128)(2,1)S(1)}, bf16[128,4096]{1,0:T(8,128)(2,1)}, u32[]{:S(2)}) %copy-start.1) | copy-done | bytes 1048600
  49.8 4.2 %shard_map.75.own_ref = f32[1024,128]{1,0:T(8,128)} custom-call(bf16[128,4096]{1,0:T(8,128)(2,1)S(1)} %copy-done.1, f32[1024,128]{1,0:T(8,128)S(1)} %bitcast.5, f32[128,8]{1,0:T(8,128)S(1)} %copy.17.baseline_ref, f32[128,8]{1,0:T(8,128)S(1)} %copy.13.gains_ref), custom_call_target="tpu_custom_call" | custom-call | flops 4000000000 | bytes 3000000 | tf_op jit(solution)/shard_map/pallas_call | solution.py:154
  54.0 8.4 %collective-permute-done.tail_ref = f32[1024,32]{1,0:T(8,128)S(1)} collective-permute-done((f32[1024,32]{1,0:T(8,128)S(1)}, f32[1024,32]{1,0:T(8,128)S(1)}, u32[]{:S(2)}, u32[]{:S(2)}) %collective-permute-start) | collective-permute-done | bytes 131104 | tf_op jit(solution)/shard_map/ppermute | solution.py:202
  62.4 3.4 %shard_map.76 = f32[1024,128]{1,0:T(8,128)} custom-call(bf16[128,4096]{1,0:T(8,128)(2,1)S(1)} %copy-done.1, f32[1024,32]{1,0:T(8,128)S(1)} %collective-permute-done.tail_ref, f32[128,8]{1,0:T(8,128)S(1)} %copy.17.baseline_ref, f32[128,8]{1,0:T(8,128)S(1)} %broadcast_multiply_fusion.gains_ref, ...), custom_call_target="tpu_custom_call", output_to_operand_aliasing={{}: (4, {})} | custom-call | flops 1000000000 | bytes 2000000 | tf_op jit(solution)/shard_map/pallas_call | solution.py:190
  (1 shorter events, 0.0 us)
Async XLA Ops:
  0.0 1.6 %copy-start = (bf16[2,2,512,512]{3,2,1,0:T(8,128)(2,1)S(1)}, bf16[2,2,512,512]{3,2,1,0:T(8,128)(2,1)}, u32[]{:S(2)}) copy-start(bf16[2,2,512,512]{3,2,1,0:T(8,128)(2,1)} %w_ref.1) | copy-start | bytes 6291460
  1.6 28.4 %copy-start.2 = (f32[128,8]{0,1:T(8,128)S(1)}, f32[128,8]{0,1:T(8,128)}, u32[]{:S(2)}) copy-start(f32[128,8]{0,1:T(8,128)} %param.10) | copy-start | bytes 12292
  1.6 28.5 %copy-start.3 = (f32[128,8]{0,1:T(8,128)S(1)}, f32[128,8]{0,1:T(8,128)}, u32[]{:S(2)}) copy-start(f32[128,8]{0,1:T(8,128)} %param.9) | copy-start | bytes 12292
  17.0 30.3 %all-to-all-start = ((f32[64,16,128]{2,1,0:T(8,128)}), f32[64,16,128]{2,1,0:T(8,128)S(1)}, u32[]{:S(2)}, u32[]{:S(2)}) async-start(f32[64,16,128]{2,1,0:T(8,128)} %shard_map.74), calls=%async_computation | async-start | bytes 1048576 | tf_op jit(solution)/shard_map/all_to_all | solution.py:207
  47.3 15.1 %collective-permute-start = (f32[1024,32]{1,0:T(8,128)S(1)}, f32[1024,32]{1,0:T(8,128)S(1)}, u32[]{:S(2)}, u32[]{:S(2)}) collective-permute-start(f32[1024,32]{1,0:T(8,128)S(1)} %bitcast.4), channel_id=1, source_target_pairs={{1,0},{2,1},{3,2},{5,4},{6,5},{7,6},{9,8},{10,9},{11,10},{13,12},{... | collective-permute-start | bytes 393224 | tf_op jit(solution)/shard_map/ppermute | solution.py:202
  48.6 1.2 %copy-start.1 = (bf16[128,4096]{1,0:T(8,128)(2,1)S(1)}, bf16[128,4096]{1,0:T(8,128)(2,1)}, u32[]{:S(2)}) copy-start(bf16[128,4096]{1,0:T(8,128)(2,1)} %shard_map.73.taps_ref) | copy-start | bytes 3145732

commit v2 on v1

v2 whole, which is shorter than its diff:
```python
import functools
import jax
import jax.numpy as jnp
from jax import lax
from jax.experimental import pallas as pl
from jax.experimental.pallas import tpu as pltpu
from jax.sharding import PartitionSpec as P

LANES = 128
F32 = jnp.float32
BF16 = jnp.bfloat16
def fold_pair(a, b, stride):
    lane = lax.broadcasted_iota(jnp.int32, a.shape, 1)
    upper = (lane & stride) != 0
    return jnp.where(
        upper, b + pltpu.roll(b, stride, 1), a + pltpu.roll(a, LANES - stride, 1)
    )


def fold(tiles, stride):
    while len(tiles) > 1:
        tiles = [fold_pair(tiles[i], tiles[i + 1], stride) for i in range(0, len(tiles), 2)]
        stride *= 2
    return tiles[0]


def beamform_kernel(chunk, width, late, v_hbm, w_hbm, out_ref, volts, weights, part, sem):
    channels, feeds, samples = v_hbm.shape[1:]
    beams = w_hbm.shape[2]
    steps = samples // width
    copies = {}
    count = 0
    for c in range(channels):
        copies[c, "w"] = pltpu.make_async_copy(w_hbm.at[:, c], weights.at[:, c], sem.at[count])
        count += 1
        if c == 0:
            for i in range(steps):
                here = pl.ds(i * width, width)
                copies[c, i] = pltpu.make_async_copy(v_hbm.at[:, c, :, here], volts.at[:, c, :, here], sem.at[count])
                count += 1
        else:
            copies[c, 0] = pltpu.make_async_copy(v_hbm.at[:, c], volts.at[:, c], sem.at[count])
            count += 1
    for copy in copies.values():
        copy.start()

    lane = lax.broadcasted_iota(jnp.int32, (chunk, LANES), 1)
    source = ((lane & 7) << 4) | (lane >> 3)

    def detect(c, i, r, both):
        real, imag = both[:chunk], both[chunk:]
        power = real * real + imag * imag
        piece = fold([power[:, k : k + LANES] for k in range(0, width, LANES)], 1)
        if i < steps - 1:
            part[i, r : r + chunk, :] = piece
            return
        tiles = [part[k, r : r + chunk, :] for k in range(steps - 1)] + [piece]
        total = jnp.take_along_axis(fold(tiles, width // LANES), source, axis=1)
        out_ref[r // 8 : (r + chunk) // 8, 8 * c : 8 * c + 8, :] = total.reshape(chunk // 8, 8, LANES)

    waiting = []
    for c in range(channels):
        copies[c, "w"].wait()
        for i in range(steps):
            if (c, i) in copies:
                copies[c, i].wait()
            right = volts[:, c, :, i * width : (i + 1) * width].reshape(2 * feeds, width)
            for r in range(0, beams, chunk):
                w0, w1 = weights[0, c, r : r + chunk, :], weights[1, c, r : r + chunk, :]
                left = jnp.concatenate(
                    [jnp.concatenate([w0, -w1], axis=1), jnp.concatenate([w1, w0], axis=1)], axis=0
                )
                both = jnp.dot(left, right, preferred_element_type=F32)
                waiting.append((c, i, r, both))
                if len(waiting) > late:
                    detect(*waiting.pop(0))
    for item in waiting:
        detect(*item)


def beamform(voltages, weights, chunk=256, width=512, late=1):
    _, channels, feeds, samples = voltages.shape
    beams = weights.shape[2]
    return pl.pallas_call(
        functools.partial(beamform_kernel, chunk, width, late),
        in_specs=[pl.BlockSpec(memory_space=pl.ANY)] * 2,
        out_shape=jax.ShapeDtypeStruct((beams // 8, 8 * channels, LANES), F32),
        scratch_shapes=[
            pltpu.VMEM(voltages.shape, BF16),
            pltpu.VMEM(weights.shape, BF16),
            pltpu.VMEM((samples // width - 1, beams, LANES), F32),
            pltpu.SemaphoreType.DMA((16,)),
        ],
        compiler_params=pltpu.CompilerParams(vmem_limit_bytes=56 * 1024 * 1024),
    )(voltages, weights)


LEVELS = 4
TREE = 16
TAPS = 32
VMEM = 24 * 1024 * 1024


def taps_kernel(offsets_ref, shifts_ref, delays_ref, taps_ref):
    rows = lax.broadcasted_iota(jnp.int32, (LANES, LANES), 0)
    cols = lax.broadcasted_iota(jnp.int32, (LANES, LANES), 1)
    tree_row = rows & (TREE - 1)
    delay = jnp.broadcast_to(offsets_ref[...], (LANES, LANES)).astype(F32)
    for level in range(LEVELS):
        half = 2**level
        block = 2 * half
        here = (cols & (block - 1)) == (tree_row >> (LEVELS - 1 - level))
        held = jnp.where(here, shifts_ref[level : level + 1, :], 0).astype(F32).astype(BF16)
        reach = ((rows >> (level + 1)) == (cols >> (level + 1))) & ((cols & half) != 0)
        delay += jnp.dot(held, jnp.where(reach, 1.0, 0.0).astype(BF16), preferred_element_type=F32)
    groups = delays_ref.shape[1]
    row8 = lax.broadcasted_iota(jnp.int32, (groups, LANES), 0)
    col8 = lax.broadcasted_iota(jnp.int32, (groups, LANES), 1)
    of_group = jnp.where(row8 == (col8 >> LEVELS), 1.0, 0.0).astype(BF16)
    spread = jnp.dot(
        delays_ref[...].astype(F32).astype(BF16), of_group, preferred_element_type=F32
    )
    delay = delay.reshape(groups, TREE, LANES) + spread.reshape(groups, 1, LANES)
    delay = delay.reshape(LANES, LANES).astype(jnp.int32)
    for d in range(TAPS):
        taps_ref[:, d * LANES : (d + 1) * LANES] = jnp.where(delay == d, 1.0, 0.0).astype(BF16)


def make_taps(offsets, shifts, delays):
    return pl.pallas_call(
        taps_kernel,
        out_shape=pltpu.VMEM((LANES, TAPS * LANES), BF16),
        cost_estimate=pl.CostEstimate(flops=4_000_000, bytes_accessed=1_100_000, transcendentals=0),
    )(offsets.reshape(1, LANES), shifts, delays)


def normalize_kernel(binned_ref, baseline_ref, gains_ref, series_ref, head_ref):
    beams = baseline_ref.shape[1]
    per = LANES // TAPS
    baseline = baseline_ref[...]
    gains = gains_ref[...]
    heads = []
    for b in range(beams):
        x = binned_ref[pl.ds(b, LANES, stride=beams), :]
        x = ((x - baseline[:, b : b + 1]) * gains[:, b : b + 1]).astype(BF16)
        series_ref[b] = x
        heads.append(x.astype(F32)[:, :TAPS])
    for j in range(beams // per):
        head_ref[j] = jnp.concatenate(heads[j * per : (j + 1) * per], axis=1).astype(BF16)


def normalize(binned, baseline, gains):
    channels, beams = baseline.shape
    groups = beams * TAPS // LANES
    return pl.pallas_call(
        normalize_kernel,
        out_shape=(
            pltpu.VMEM((beams, channels, LANES), BF16),
            pltpu.VMEM((groups, channels, LANES), BF16),
        ),
        compiler_params=pltpu.CompilerParams(vmem_limit_bytes=VMEM),
        cost_estimate=pl.CostEstimate(flops=1_000_000, bytes_accessed=600_000, transcendentals=0),
    )(binned.reshape(channels * beams, LANES), baseline, gains)


def own_kernel(taps_ref, series_ref, out_ref, *windows):
    beams = series_ref.shape[0]
    lane = lax.broadcasted_iota(jnp.int32, (LANES, LANES), 1)
    for pair in range(beams // 2):
        window = windows[pair % len(windows)]
        for j in range(2):
            x = series_ref[2 * pair + j].astype(F32)
            for d in range(TAPS):
                moved = x if d == 0 else jnp.where(lane < LANES - d, pltpu.roll(x, LANES - d, 1), 0.0)
                window[d * LANES : (d + 1) * LANES, j * LANES : (j + 1) * LANES] = moved.astype(BF16)
        both = jnp.dot(taps_ref[...], window[...], preferred_element_type=F32)
        for j in range(2):
            out_ref[pl.ds(2 * pair + j, LANES, stride=beams), :] = both[:, j * LANES : (j + 1) * LANES]


def dedisperse_own(taps, series):
    beams = series.shape[0]
    return pl.pallas_call(
        own_kernel,
        out_shape=pltpu.VMEM((LANES * beams, LANES), F32),
        in_specs=[pl.BlockSpec(memory_space=pltpu.VMEM)] * 2,
        scratch_shapes=[pltpu.VMEM((TAPS * LANES, 2 * LANES), BF16)] * 2,
        compiler_params=pltpu.CompilerParams(vmem_limit_bytes=VMEM),
        cost_estimate=pl.CostEstimate(flops=4_000_000_000, bytes_accessed=3_000_000, transcendentals=0),
    )(taps, series)


def tail_kernel(taps_ref, tail_ref, own_ref, out_ref, window):
    groups = tail_ref.shape[0]
    per = LANES // TAPS
    beams = groups * per
    lane = lax.broadcasted_iota(jnp.int32, (LANES, LANES), 1)
    for j in range(groups):
        x = tail_ref[j].astype(F32)
        for d in range(TAPS):
            keep = (lane & (TAPS - 1)) >= TAPS - d
            moved = jnp.where(keep, pltpu.roll(x, (TAPS - d) % LANES, 1), 0.0)
            window[d * LANES : (d + 1) * LANES, j * LANES : (j + 1) * LANES] = moved.astype(BF16)
    added = jnp.dot(taps_ref[...], window[...], preferred_element_type=F32)
    last = lane >= LANES - TAPS
    for b in range(beams):
        rows = pl.ds(b, LANES, stride=beams)
        j, i = divmod(b, per)
        piece = added[:, j * LANES : (j + 1) * LANES]
        piece = pltpu.roll(piece, (per - 1 - i) * TAPS, 1)
        out_ref[rows, :] = own_ref[rows, :] + jnp.where(last, piece, 0.0)


def add_tail(taps, tail, own):
    return pl.pallas_call(
        tail_kernel,
        out_shape=jax.ShapeDtypeStruct(own.shape, F32),
        in_specs=[pl.BlockSpec(memory_space=pltpu.VMEM)] * 3,
        scratch_shapes=[pltpu.VMEM((TAPS * LANES, 2 * LANES), BF16)],
        compiler_params=pltpu.CompilerParams(vmem_limit_bytes=VMEM),
        cost_estimate=pl.CostEstimate(flops=1_000_000_000, bytes_accessed=2_000_000, transcendentals=0),
    )(taps, tail, own)


def from_behind(value, axis):
    count = lax.axis_size(axis)
    return lax.ppermute(value, axis, [(source, source - 1) for source in range(1, count)])


def per_device(voltages, weights, baseline, gains, offsets, shifts, delays):
    channels, beams = baseline.shape
    binned = beamform(voltages, weights)
    received = lax.all_to_all(binned, "chan", split_axis=0, concat_axis=0, tiled=True)
    taps = make_taps(offsets, shifts, delays)
    series, head = normalize(received, baseline, gains)
    following = from_behind(head, "tm")
    own = dedisperse_own(taps, series)
    return add_tail(taps, following, own).reshape(channels, beams, LANES)


def solution(mesh):
    placed = (
        P(None, "chan", None, "tm"),
        P(None, "chan", None, None),
        P(None, "chan"),
        P(None, "chan"),
        P(),
        P(),
        P(),
    )
    return jax.shard_map(
        per_device, mesh=mesh, in_specs=placed, out_specs=P(None, "chan", "tm"), check_vma=False
    )
```

time: 66.1 us -> 50.4 us (0.76)
  Pallas kernels: 25.2 us -> 18.6 us
  waiting for transfers between devices: 23.3 us -> 16.8 us
  local copies, waits for them, and re-layouts: 3.02 us -> 0.21 us
    ppermute x1, waiting for transfers between devices: 8.37 us -> 0.95 us  [from_behind(): lax.ppermute(value, axis, [(source, source - 1) for source in range(1, co...]
    pallas_call x4 -> x5, Pallas kernels: 25.2 us -> 18.6 us  [the longest x1 12.5 us: beamform(): pl.pallas_call(functools.partial(beamform_kernel, chunk, width, late), in...]
    unnamed x10 -> x6, local copies, waits for them, and re-layouts: 3.02 us -> 0.21 us
    all_to_all x1, waiting for transfers between devices: 14.9 us -> 15.9 us  [per_device(): lax.all_to_all(binned, 'chan', split_axis=0, concat_axis=0, tiled=True)]
  transfers between devices with their start and end apart: 2 -> 2, of which waited for: 2 -> 2; matrix products, arithmetic and copies ran while one was open for 0% -> 0% of each run, Pallas kernels for 10% -> 8%
where the time goes in v2:
time: 50.4 us; the launch traced here: 50.1 us
  Pallas kernels  18.6 us (37%)
  waiting for transfers between devices  16.8 us (33%)
  starting transfers between devices  14.5 us (29%)
    all_to_all x1, waiting for transfers between devices, per_device(): lax.all_to_all(binned, 'chan', split_axis=0, concat_axis=0, tiled=True)  15.9 us
    all_to_all x1, starting transfers between devices, per_device(): lax.all_to_all(binned, 'chan', split_axis=0, concat_axis=0, tiled=True)  13 us
    pallas_call x1, Pallas kernels, beamform(): pl.pallas_call(functools.partial(beamform_kernel, chunk, width, late), in...  12.5 us
    pallas_call x1, Pallas kernels, dedisperse_own(): pl.pallas_call(own_kernel, out_shape=pltpu.VMEM((LANES * beams, LANES), F...  2.57 us
    pallas_call x1, Pallas kernels, add_tail(): pl.pallas_call(tail_kernel, out_shape=jax.ShapeDtypeStruct(own.shape, F32...  1.85 us
    ppermute x1, starting transfers between devices, from_behind(): lax.ppermute(value, axis, [(source, source - 1) for source in range(1, co...  1.47 us
    pallas_call x1, Pallas kernels, make_taps(): pl.pallas_call(taps_kernel, out_shape=pltpu.VMEM((LANES, TAPS * LANES), B...  1.23 us
  transfers between devices with their start and end apart: 2, of which 2 were waited for; matrix products, arithmetic and copies ran while one was open for 0% of the time, Pallas kernels for 8%

profile of v2, /device:TPU:1, one launch (start us, length us, event | category | flops | bytes accessed | tf_op | source)
XLA Modules:
  0.0 50.1 jit_solution(7844626602107305949)
XLA Ops:
  0.0 0.0 copy-start
  0.0 0.0 copy-start.1
  0.0 12.5 %shard_map.74 = f32[64,16,128]{2,1,0:T(8,128)} custom-call(bf16[2,2,512,2048]{3,2,1,0:T(8,128)(2,1)} %v_hbm.1, bf16[2,2,512,512]{3,2,1,0:T(8,128)(2,1)} %w_hbm.1), custom_call_target="tpu_custom_call" | custom-call | tf_op jit(solution)/shard_map/pallas_call | solution.py:84
  12.5 13.0 %all-to-all-start = ((f32[64,16,128]{2,1,0:T(8,128)}), f32[64,16,128]{2,1,0:T(8,128)S(1)}, u32[]{:S(2)}, u32[]{:S(2)}) async-start(f32[64,16,128]{2,1,0:T(8,128)} %shard_map.74), calls=%async_computation | async-start | bytes 1048576 | tf_op jit(solution)/shard_map/all_to_all | solution.py:233
  25.5 0.0 copy-done
  25.5 0.1 copy.8.baseline_ref
  25.6 0.0 copy-done.1
  25.6 0.1 copy.9.gains_ref
  25.7 1.2 %shard_map.73.taps_ref = bf16[128,4096]{1,0:T(8,128)(2,1)S(1)} custom-call(s32[1,128]{1,0:T(1,128)} %bitcast.4, s32[4,128]{1,0:T(4,128)} %shifts_ref.1, s32[8,8]{1,0:T(8,128)} %delays_ref.1), custom_call_target="tpu_custom_call" | custom-call | flops 4000000 | bytes 1100000 | tf_op jit(solution)/shard_map/pallas_call | solution.py:130
  27.0 15.9 %all-to-all-done = f32[64,16,128]{2,1,0:T(8,128)S(1)} async-done(((f32[64,16,128]{2,1,0:T(8,128)}), f32[64,16,128]{2,1,0:T(8,128)S(1)}, u32[]{:S(2)}, u32[]{:S(2)}) %all-to-all-start) | async-done | bytes 524320 | tf_op jit(solution)/shard_map/all_to_all | solution.py:233
  42.8 0.4 shard_map.75
  43.3 1.5 %collective-permute-start = (bf16[2,128,128]{2,1,0:T(8,128)(2,1)S(1)}, bf16[2,128,128]{2,1,0:T(8,128)(2,1)S(1)}, u32[]{:S(2)}, u32[]{:S(2)}) collective-permute-start(bf16[2,128,128]{2,1,0:T(8,128)(2,1)S(1)} %get-tuple-element.7), channel_id=1, source_target_pairs={{1,0},{2,1},{3,2},{5,4},{6,5},{7,6},{9,8},{10,9},{11,10},{13,12},{... | collective-permute-start | bytes 196616 | tf_op jit(solution)/shard_map/ppermute | solution.py:227
  44.7 2.6 %shard_map.76.own_ref = f32[1024,128]{1,0:T(8,128)S(1)} custom-call(bf16[128,4096]{1,0:T(8,128)(2,1)S(1)} %shard_map.73.taps_ref, bf16[8,128,128]{2,1,0:T(8,128)(2,1)S(1)} %get-tuple-element.8.series_ref), custom_call_target="tpu_custom_call" | custom-call | flops 4000000000 | bytes 3000000 | tf_op jit(solution)/shard_map/pallas_call | solution.py:183
  47.3 1.0 %collective-permute-done.tail_ref = bf16[2,128,128]{2,1,0:T(8,128)(2,1)S(1)} collective-permute-done((bf16[2,128,128]{2,1,0:T(8,128)(2,1)S(1)}, bf16[2,128,128]{2,1,0:T(8,128)(2,1)S(1)}, u32[]{:S(2)}, u32[]{:S(2)}) %collective-permute-start) | collective-permute-done | bytes 65568 | tf_op jit(solution)/shard_map/ppermute | solution.py:227
  48.3 1.8 %shard_map.77 = f32[1024,128]{1,0:T(8,128)} custom-call(bf16[128,4096]{1,0:T(8,128)(2,1)S(1)} %shard_map.73.taps_ref, bf16[2,128,128]{2,1,0:T(8,128)(2,1)S(1)} %collective-permute-done.tail_ref, f32[1024,128]{1,0:T(8,128)S(1)} %shard_map.76.own_ref), custom_call_target="tpu_custom_call" | custom-call | flops 1000000000 | bytes 2000000 | tf_op jit(solution)/shard_map/pallas_call | solution.py:215
Async XLA Ops:
  0.0 25.5 %copy-start = (f32[128,8]{0,1:T(8,128)S(1)}, f32[128,8]{0,1:T(8,128)}, u32[]{:S(2)}) copy-start(f32[128,8]{0,1:T(8,128)} %param.9) | copy-start | bytes 12292
  0.0 25.6 %copy-start.1 = (f32[128,8]{0,1:T(8,128)S(1)}, f32[128,8]{0,1:T(8,128)}, u32[]{:S(2)}) copy-start(f32[128,8]{0,1:T(8,128)} %param.10) | copy-start | bytes 12292
  12.5 30.3 %all-to-all-start = ((f32[64,16,128]{2,1,0:T(8,128)}), f32[64,16,128]{2,1,0:T(8,128)S(1)}, u32[]{:S(2)}, u32[]{:S(2)}) async-start(f32[64,16,128]{2,1,0:T(8,128)} %shard_map.74), calls=%async_computation | async-start | bytes 1048576 | tf_op jit(solution)/shard_map/all_to_all | solution.py:233
  43.3 5.0 %collective-permute-start = (bf16[2,128,128]{2,1,0:T(8,128)(2,1)S(1)}, bf16[2,128,128]{2,1,0:T(8,128)(2,1)S(1)}, u32[]{:S(2)}, u32[]{:S(2)}) collective-permute-start(bf16[2,128,128]{2,1,0:T(8,128)(2,1)S(1)} %get-tuple-element.7), channel_id=1, source_target_pairs={{1,0},{2,1},{3,2},{5,4},{6,5},{7,6},{9,8},{10,9},{11,10},{13,12},{... | collective-permute-start | bytes 196616 | tf_op jit(solution)/shard_map/ppermute | solution.py:227

commit v3 on v2

--- a/solution.py
+++ b/solution.py
@@ -9,6 +9,10 @@
 LANES = 128
 F32 = jnp.float32
 BF16 = jnp.bfloat16
+CENTRE = 32.0
+SCALE = 2.0**-10
+
+
 def fold_pair(a, b, stride):
     lane = lax.broadcasted_iota(jnp.int32, a.shape, 1)
     upper = (lane & stride) != 0
@@ -24,7 +28,20 @@
     return tiles[0]
 
 
-def beamform_kernel(chunk, width, late, v_hbm, w_hbm, out_ref, volts, weights, part, sem):
+def encode(binned):
+    x = (binned - CENTRE) * SCALE
+    square = x * x
+    fourth = square * square
+    eighth = fourth * fourth
+    return jnp.where(x < 0.0, -eighth, eighth)
+
+
+def decode(code):
+    root = jnp.sqrt(jnp.sqrt(jnp.sqrt(jnp.abs(code)))) * (1.0 / SCALE)
+    return jnp.where(code < 0.0, -root, root)
+
+
+def beamform_kernel(chunk, width, late, v_hbm, w_hbm, out_ref, volts, weights, part, done, sem):
     channels, feeds, samples = v_hbm.shape[1:]
     beams = w_hbm.shape[2]
     steps = samples // width
@@ -34,8 +51,8 @@
         copies[c, "w"] = pltpu.make_async_copy(w_hbm.at[:, c], weights.at[:, c], sem.at[count])
         count += 1
         if c == 0:
-            for i in range(steps):
-                here = pl.ds(i * width, width)
+            for i, lanes in ((0, width), (1, samples - width)):
+                here = pl.ds(i * width, lanes)
                 copies[c, i] = pltpu.make_async_copy(v_hbm.at[:, c, :, here], volts.at[:, c, :, here], sem.at[count])
                 count += 1
         else:
@@ -56,7 +73,10 @@
             return
         tiles = [part[k, r : r + chunk, :] for k in range(steps - 1)] + [piece]
         total = jnp.take_along_axis(fold(tiles, width // LANES), source, axis=1)
-        out_ref[r // 8 : (r + chunk) // 8, 8 * c : 8 * c + 8, :] = total.reshape(chunk // 8, 8, LANES)
+        done[c, r : r + chunk, :] = encode(total)
+        if c == channels - 1:
+            blocks = [done[k, r : r + chunk, :].reshape(chunk // 8, 8, LANES) for k in range(channels)]
+            out_ref[r // 8 : (r + chunk) // 8] = jnp.concatenate(blocks, axis=1).astype(BF16)
 
     waiting = []
     for c in range(channels):
@@ -84,11 +104,12 @@
     return pl.pallas_call(
         functools.partial(beamform_kernel, chunk, width, late),
         in_specs=[pl.BlockSpec(memory_space=pl.ANY)] * 2,
-        out_shape=jax.ShapeDtypeStruct((beams // 8, 8 * channels, LANES), F32),
+        out_shape=jax.ShapeDtypeStruct((beams // 8, 8 * channels, LANES), BF16),
         scratch_shapes=[
             pltpu.VMEM(voltages.shape, BF16),
             pltpu.VMEM(weights.shape, BF16),
             pltpu.VMEM((samples // width - 1, beams, LANES), F32),
+            pltpu.VMEM((channels, beams, LANES), F32),
             pltpu.SemaphoreType.DMA((16,)),
         ],
         compiler_params=pltpu.CompilerParams(vmem_limit_bytes=56 * 1024 * 1024),
@@ -134,22 +155,23 @@
     )(offsets.reshape(1, LANES), shifts, delays)
 
 
-def normalize_kernel(binned_ref, baseline_ref, gains_ref, series_ref, head_ref):
+def normalize_kernel(received_ref, baseline_ref, gains_ref, series_ref, head_ref, wide):
     beams = baseline_ref.shape[1]
     per = LANES // TAPS
-    baseline = baseline_ref[...]
+    wide[...] = decode(received_ref[...].astype(F32)).reshape(wide.shape)
+    above = baseline_ref[...] - CENTRE
     gains = gains_ref[...]
     heads = []
     for b in range(beams):
-        x = binned_ref[pl.ds(b, LANES, stride=beams), :]
-        x = ((x - baseline[:, b : b + 1]) * gains[:, b : b + 1]).astype(BF16)
+        x = wide[pl.ds(b, LANES, stride=beams), :]
+        x = ((x - above[:, b : b + 1]) * gains[:, b : b + 1]).astype(BF16)
         series_ref[b] = x
         heads.append(x.astype(F32)[:, :TAPS])
     for j in range(beams // per):
         head_ref[j] = jnp.concatenate(heads[j * per : (j + 1) * per], axis=1).astype(BF16)
 
 
-def normalize(binned, baseline, gains):
+def normalize(received, baseline, gains):
     channels, beams = baseline.shape
     groups = beams * TAPS // LANES
     return pl.pallas_call(
@@ -158,9 +180,10 @@
             pltpu.VMEM((beams, channels, LANES), BF16),
             pltpu.VMEM((groups, channels, LANES), BF16),
         ),
+        scratch_shapes=[pltpu.VMEM((channels * beams, LANES), F32)],
         compiler_params=pltpu.CompilerParams(vmem_limit_bytes=VMEM),
         cost_estimate=pl.CostEstimate(flops=1_000_000, bytes_accessed=600_000, transcendentals=0),
-    )(binned.reshape(channels * beams, LANES), baseline, gains)
+    )(received, baseline, gains)
 
 
 def own_kernel(taps_ref, series_ref, out_ref, *windows):
@@ -229,8 +252,8 @@
 
 def per_device(voltages, weights, baseline, gains, offsets, shifts, delays):
     channels, beams = baseline.shape
-    binned = beamform(voltages, weights)
-    received = lax.all_to_all(binned, "chan", split_axis=0, concat_axis=0, tiled=True)
+    codes = beamform(voltages, weights)
+    received = lax.all_to_all(codes, "chan", split_axis=0, concat_axis=0, tiled=True)
     taps = make_taps(offsets, shifts, delays)
     series, head = normalize(received, baseline, gains)
     following = from_behind(head, "tm")

time: 50.4 us -> 45.1 us (0.89)
  waiting for transfers between devices: 16.8 us -> 11.5 us
    all_to_all x1, waiting for transfers between devices: 15.9 us -> 10.5 us  [per_device(): lax.all_to_all(codes, 'chan', split_axis=0, concat_axis=0, tiled=True)]
where the time goes in v3:
time: 45.1 us; the launch traced here: 44.8 us
  Pallas kernels  18.5 us (41%)
  starting transfers between devices  14.5 us (32%)
  waiting for transfers between devices  11.5 us (25%)
    all_to_all x1, starting transfers between devices, per_device(): lax.all_to_all(codes, 'chan', split_axis=0, concat_axis=0, tiled=True)  13 us
    pallas_call x1, Pallas kernels, beamform(): pl.pallas_call(functools.partial(beamform_kernel, chunk, width, late), in...  12.1 us
    all_to_all x1, waiting for transfers between devices, per_device(): lax.all_to_all(codes, 'chan', split_axis=0, concat_axis=0, tiled=True)  10.5 us
    pallas_call x1, Pallas kernels, dedisperse_own(): pl.pallas_call(own_kernel, out_shape=pltpu.VMEM((LANES * beams, LANES), F...  2.57 us
    pallas_call x1, Pallas kernels, add_tail(): pl.pallas_call(tail_kernel, out_shape=jax.ShapeDtypeStruct(own.shape, F32...  1.85 us
    ppermute x1, starting transfers between devices, from_behind(): lax.ppermute(value, axis, [(source, source - 1) for source in range(1, co...  1.47 us
    pallas_call x1, Pallas kernels, make_taps(): pl.pallas_call(taps_kernel, out_shape=pltpu.VMEM((LANES, TAPS * LANES), B...  1.23 us
    ppermute x1, waiting for transfers between devices, from_behind(): lax.ppermute(value, axis, [(source, source - 1) for source in range(1, co...  0.95 us
  transfers between devices with their start and end apart: 2, of which 2 were waited for; matrix products, arithmetic and copies ran while one was open for 0% of the time, Pallas kernels for 8%

profile of v3, /device:TPU:1, one launch (start us, length us, event | category | flops | bytes accessed | tf_op | source)
XLA Modules:
  0.0 44.8 jit_solution(1802049689480489097)
XLA Ops:
  0.0 0.0 copy-start
  0.0 0.0 copy-start.1
  0.0 12.1 %shard_map.74 = bf16[64,16,128]{2,1,0:T(8,128)(2,1)} custom-call(bf16[2,2,512,2048]{3,2,1,0:T(8,128)(2,1)} %v_hbm.1, bf16[2,2,512,512]{3,2,1,0:T(8,128)(2,1)} %w_hbm.1), custom_call_target="tpu_custom_call" | custom-call | tf_op jit(solution)/shard_map/pallas_call | solution.py:104
  12.1 13.0 %all-to-all-start = ((bf16[64,16,128]{2,1,0:T(8,128)(2,1)}), bf16[64,16,128]{2,1,0:T(8,128)(2,1)S(1)}, u32[]{:S(2)}, u32[]{:S(2)}) async-start(bf16[64,16,128]{2,1,0:T(8,128)(2,1)} %shard_map.74), calls=%async_computation | async-start | bytes 524288 | tf_op jit(solution)/shard_map/all_to_all | solution.py:256
  25.1 0.0 copy-done
  25.1 0.1 copy.8.baseline_ref
  25.2 0.0 copy-done.1
  25.2 0.1 copy.9.gains_ref
  25.3 1.2 %shard_map.73.taps_ref = bf16[128,4096]{1,0:T(8,128)(2,1)S(1)} custom-call(s32[1,128]{1,0:T(1,128)} %bitcast.2, s32[4,128]{1,0:T(4,128)} %shifts_ref.1, s32[8,8]{1,0:T(8,128)} %delays_ref.1), custom_call_target="tpu_custom_call" | custom-call | flops 4000000 | bytes 1100000 | tf_op jit(solution)/shard_map/pallas_call | solution.py:151
  26.5 10.5 %all-to-all-done.received_ref = bf16[64,16,128]{2,1,0:T(8,128)(2,1)S(1)} async-done(((bf16[64,16,128]{2,1,0:T(8,128)(2,1)}), bf16[64,16,128]{2,1,0:T(8,128)(2,1)S(1)}, u32[]{:S(2)}, u32[]{:S(2)}) %all-to-all-start) | async-done | bytes 262176 | tf_op jit(solution)/shard_map/all_to_all | solution.py:256
  37.1 0.8 %shard_map.75 = (bf16[8,128,128]{2,1,0:T(8,128)(2,1)S(1)}, bf16[2,128,128]{2,1,0:T(8,128)(2,1)S(1)}) custom-call(bf16[64,16,128]{2,1,0:T(8,128)(2,1)S(1)} %all-to-all-done.received_ref, f32[128,8]{1,0:T(8,128)S(1)} %copy.8.baseline_ref, f32[128,8]{1,0:T(8,128)S(1)} %copy.9.gains_ref), custom_call_target="tpu_custom_call" | custom-call | flops 1000000 | bytes 600000 | tf_op jit(solution)/shard_map/pallas_call | solution.py:177
  37.9 1.5 %collective-permute-start = (bf16[2,128,128]{2,1,0:T(8,128)(2,1)S(1)}, bf16[2,128,128]{2,1,0:T(8,128)(2,1)S(1)}, u32[]{:S(2)}, u32[]{:S(2)}) collective-permute-start(bf16[2,128,128]{2,1,0:T(8,128)(2,1)S(1)} %get-tuple-element.7), channel_id=1, source_target_pairs={{1,0},{2,1},{3,2},{5,4},{6,5},{7,6},{9,8},{10,9},{11,10},{13,12},{... | collective-permute-start | bytes 196616 | tf_op jit(solution)/shard_map/ppermute | solution.py:250
  39.4 2.6 %shard_map.76.own_ref = f32[1024,128]{1,0:T(8,128)S(1)} custom-call(bf16[128,4096]{1,0:T(8,128)(2,1)S(1)} %shard_map.73.taps_ref, bf16[8,128,128]{2,1,0:T(8,128)(2,1)S(1)} %get-tuple-element.8.series_ref), custom_call_target="tpu_custom_call" | custom-call | flops 4000000000 | bytes 3000000 | tf_op jit(solution)/shard_map/pallas_call | solution.py:206
  42.0 1.0 %collective-permute-done.tail_ref = bf16[2,128,128]{2,1,0:T(8,128)(2,1)S(1)} collective-permute-done((bf16[2,128,128]{2,1,0:T(8,128)(2,1)S(1)}, bf16[2,128,128]{2,1,0:T(8,128)(2,1)S(1)}, u32[]{:S(2)}, u32[]{:S(2)}) %collective-permute-start) | collective-permute-done | bytes 65568 | tf_op jit(solution)/shard_map/ppermute | solution.py:250
  42.9 1.8 %shard_map.77 = f32[1024,128]{1,0:T(8,128)} custom-call(bf16[128,4096]{1,0:T(8,128)(2,1)S(1)} %shard_map.73.taps_ref, bf16[2,128,128]{2,1,0:T(8,128)(2,1)S(1)} %collective-permute-done.tail_ref, f32[1024,128]{1,0:T(8,128)S(1)} %shard_map.76.own_ref), custom_call_target="tpu_custom_call" | custom-call | flops 1000000000 | bytes 2000000 | tf_op jit(solution)/shard_map/pallas_call | solution.py:238
Async XLA Ops:
  0.0 25.1 %copy-start = (f32[128,8]{0,1:T(8,128)S(1)}, f32[128,8]{0,1:T(8,128)}, u32[]{:S(2)}) copy-start(f32[128,8]{0,1:T(8,128)} %param.9) | copy-start | bytes 12292
  0.0 25.2 %copy-start.1 = (f32[128,8]{0,1:T(8,128)S(1)}, f32[128,8]{0,1:T(8,128)}, u32[]{:S(2)}) copy-start(f32[128,8]{0,1:T(8,128)} %param.10) | copy-start | bytes 12292
  12.1 25.0 %all-to-all-start = ((bf16[64,16,128]{2,1,0:T(8,128)(2,1)}), bf16[64,16,128]{2,1,0:T(8,128)(2,1)S(1)}, u32[]{:S(2)}, u32[]{:S(2)}) async-start(bf16[64,16,128]{2,1,0:T(8,128)(2,1)} %shard_map.74), calls=%async_computation | async-start | bytes 524288 | tf_op jit(solution)/shard_map/all_to_all | solution.py:256
  37.9 5.0 %collective-permute-start = (bf16[2,128,128]{2,1,0:T(8,128)(2,1)S(1)}, bf16[2,128,128]{2,1,0:T(8,128)(2,1)S(1)}, u32[]{:S(2)}, u32[]{:S(2)}) collective-permute-start(bf16[2,128,128]{2,1,0:T(8,128)(2,1)S(1)} %get-tuple-element.7), channel_id=1, source_target_pairs={{1,0},{2,1},{3,2},{5,4},{6,5},{7,6},{9,8},{10,9},{11,10},{13,12},{... | collective-permute-start | bytes 196616 | tf_op jit(solution)/shard_map/ppermute | solution.py:250

commit v4 on v3

--- a/solution.py
+++ b/solution.py
@@ -37,7 +37,7 @@
 
 
 def decode(code):
-    root = jnp.sqrt(jnp.sqrt(jnp.sqrt(jnp.abs(code)))) * (1.0 / SCALE)
+    root = jnp.exp2(jnp.log2(jnp.abs(code)) * 0.125) * (1.0 / SCALE)
     return jnp.where(code < 0.0, -root, root)
 
 
@@ -155,44 +155,55 @@
     )(offsets.reshape(1, LANES), shifts, delays)
 
 
-def normalize_kernel(received_ref, baseline_ref, gains_ref, series_ref, head_ref, wide):
+def head_kernel(codes_ref, baseline_ref, gains_ref, head_ref, wide):
     beams = baseline_ref.shape[1]
     per = LANES // TAPS
-    wide[...] = decode(received_ref[...].astype(F32)).reshape(wide.shape)
+    wide[...] = codes_ref[...].astype(F32).reshape(wide.shape)
     above = baseline_ref[...] - CENTRE
     gains = gains_ref[...]
-    heads = []
-    for b in range(beams):
-        x = wide[pl.ds(b, LANES, stride=beams), :]
-        x = ((x - above[:, b : b + 1]) * gains[:, b : b + 1]).astype(BF16)
-        series_ref[b] = x
-        heads.append(x.astype(F32)[:, :TAPS])
+    lane = lax.broadcasted_iota(jnp.int32, (LANES, LANES), 1)
     for j in range(beams // per):
-        head_ref[j] = jnp.concatenate(heads[j * per : (j + 1) * per], axis=1).astype(BF16)
-
-
-def normalize(received, baseline, gains):
+        packed, floor, gain = None, None, None
+        for i in range(per):
+            b = j * per + i
+            x = wide[pl.ds(b, LANES, stride=beams), :]
+            x = x if i == 0 else pltpu.roll(x, i * TAPS, 1)
+            low = jnp.broadcast_to(above[:, b : b + 1], x.shape)
+            up = jnp.broadcast_to(gains[:, b : b + 1], x.shape)
+            if i == 0:
+                packed, floor, gain = x, low, up
+            else:
+                here = lane >= i * TAPS
+                packed = jnp.where(here, x, packed)
+                floor = jnp.where(here, low, floor)
+                gain = jnp.where(here, up, gain)
+        head_ref[j] = ((decode(packed) - floor) * gain).astype(BF16)
+
+
+def make_head(codes, baseline, gains):
     channels, beams = baseline.shape
-    groups = beams * TAPS // LANES
-    return pl.pallas_call(
-        normalize_kernel,
-        out_shape=(
-            pltpu.VMEM((beams, channels, LANES), BF16),
-            pltpu.VMEM((groups, channels, LANES), BF16),
-        ),
+    return pl.pallas_call(
+        head_kernel,
+        out_shape=pltpu.VMEM((beams * TAPS // LANES, channels, LANES), BF16),
         scratch_shapes=[pltpu.VMEM((channels * beams, LANES), F32)],
         compiler_params=pltpu.CompilerParams(vmem_limit_bytes=VMEM),
-        cost_estimate=pl.CostEstimate(flops=1_000_000, bytes_accessed=600_000, transcendentals=0),
-    )(received, baseline, gains)
-
-
-def own_kernel(taps_ref, series_ref, out_ref, *windows):
-    beams = series_ref.shape[0]
+        cost_estimate=pl.CostEstimate(flops=1_000_000, bytes_accessed=400_000, transcendentals=0),
+    )(codes, baseline, gains)
+
+
+def own_kernel(taps_ref, codes_ref, baseline_ref, gains_ref, out_ref, wide, *windows):
+    beams = baseline_ref.shape[1]
+    wide[...] = codes_ref[...].astype(F32).reshape(wide.shape)
+    above = baseline_ref[...] - CENTRE
+    gains = gains_ref[...]
     lane = lax.broadcasted_iota(jnp.int32, (LANES, LANES), 1)
     for pair in range(beams // 2):
         window = windows[pair % len(windows)]
         for j in range(2):
-            x = series_ref[2 * pair + j].astype(F32)
+            b = 2 * pair + j
+            x = decode(wide[pl.ds(b, LANES, stride=beams), :])
+            x = ((x - above[:, b : b + 1]) * gains[:, b : b + 1]).astype(BF16)
+            x = x.astype(F32)
             for d in range(TAPS):
                 moved = x if d == 0 else jnp.where(lane < LANES - d, pltpu.roll(x, LANES - d, 1), 0.0)
                 window[d * LANES : (d + 1) * LANES, j * LANES : (j + 1) * LANES] = moved.astype(BF16)
@@ -201,19 +212,20 @@
             out_ref[pl.ds(2 * pair + j, LANES, stride=beams), :] = both[:, j * LANES : (j + 1) * LANES]
 
 
-def dedisperse_own(taps, series):
-    beams = series.shape[0]
+def dedisperse_own(taps, codes, baseline, gains):
+    channels, beams = baseline.shape
     return pl.pallas_call(
         own_kernel,
         out_shape=pltpu.VMEM((LANES * beams, LANES), F32),
-        in_specs=[pl.BlockSpec(memory_space=pltpu.VMEM)] * 2,
-        scratch_shapes=[pltpu.VMEM((TAPS * LANES, 2 * LANES), BF16)] * 2,
+        in_specs=[pl.BlockSpec(memory_space=pltpu.VMEM)] * 4,
+        scratch_shapes=[pltpu.VMEM((channels * beams, LANES), F32)]
+        + [pltpu.VMEM((TAPS * LANES, 2 * LANES), BF16)] * 2,
         compiler_params=pltpu.CompilerParams(vmem_limit_bytes=VMEM),
         cost_estimate=pl.CostEstimate(flops=4_000_000_000, bytes_accessed=3_000_000, transcendentals=0),
-    )(taps, series)
-
-
-def tail_kernel(taps_ref, tail_ref, own_ref, out_ref, window):
+    )(taps, codes, baseline, gains)
+
+
+def tail_kernel(taps_ref, tail_ref, own_ref, out_hbm, window, total, sem):
     groups = tail_ref.shape[0]
     per = LANES // TAPS
     beams = groups * per
@@ -225,13 +237,20 @@
             moved = jnp.where(keep, pltpu.roll(x, (TAPS - d) % LANES, 1), 0.0)
             window[d * LANES : (d + 1) * LANES, j * LANES : (j + 1) * LANES] = moved.astype(BF16)
     added = jnp.dot(taps_ref[...], window[...], preferred_element_type=F32)
-    last = lane >= LANES - TAPS
-    for b in range(beams):
-        rows = pl.ds(b, LANES, stride=beams)
-        j, i = divmod(b, per)
-        piece = added[:, j * LANES : (j + 1) * LANES]
-        piece = pltpu.roll(piece, (per - 1 - i) * TAPS, 1)
-        out_ref[rows, :] = own_ref[rows, :] + jnp.where(last, piece, 0.0)
+    last = lax.broadcasted_iota(jnp.int32, (TREE, LANES), 1) >= LANES - TAPS
+    copies = []
+    for q in range(LANES // TREE):
+        for b in range(beams):
+            rows = pl.ds(q * TREE * beams + b, TREE, stride=beams)
+            j, i = divmod(b, per)
+            piece = added[q * TREE : (q + 1) * TREE, j * LANES : (j + 1) * LANES]
+            piece = pltpu.roll(piece, (per - 1 - i) * TAPS, 1)
+            total[rows, :] = own_ref[rows, :] + jnp.where(last, piece, 0.0)
+        block = pl.ds(q * TREE * beams, TREE * beams)
+        copies.append(pltpu.make_async_copy(total.at[block], out_hbm.at[block], sem.at[q]))
+        copies[-1].start()
+    for copy in copies:
+        copy.wait()
 
 
 def add_tail(taps, tail, own):
@@ -239,7 +258,12 @@
         tail_kernel,
         out_shape=jax.ShapeDtypeStruct(own.shape, F32),
         in_specs=[pl.BlockSpec(memory_space=pltpu.VMEM)] * 3,
-        scratch_shapes=[pltpu.VMEM((TAPS * LANES, 2 * LANES), BF16)],
+        out_specs=pl.BlockSpec(memory_space=pl.ANY),
+        scratch_shapes=[
+            pltpu.VMEM((TAPS * LANES, 2 * LANES), BF16),
+            pltpu.VMEM(own.shape, F32),
+            pltpu.SemaphoreType.DMA((LANES // TREE,)),
+        ],
         compiler_params=pltpu.CompilerParams(vmem_limit_bytes=VMEM),
         cost_estimate=pl.CostEstimate(flops=1_000_000_000, bytes_accessed=2_000_000, transcendentals=0),
     )(taps, tail, own)
@@ -255,9 +279,8 @@
     codes = beamform(voltages, weights)
     received = lax.all_to_all(codes, "chan", split_axis=0, concat_axis=0, tiled=True)
     taps = make_taps(offsets, shifts, delays)
-    series, head = normalize(received, baseline, gains)
-    following = from_behind(head, "tm")
-    own = dedisperse_own(taps, series)
+    following = from_behind(make_head(received, baseline, gains), "tm")
+    own = dedisperse_own(taps, received, baseline, gains)
     return add_tail(taps, following, own).reshape(channels, beams, LANES)
 
 

time: 45.1 us -> 45 us (level)
  waiting for transfers between devices: 11.5 us -> 10.7 us
  Pallas kernels: 18.5 us -> 19 us
    ppermute x1, waiting for transfers between devices: 0.95 us -> 0.11 us  [from_behind(): lax.ppermute(value, axis, [(source, source - 1) for source in range(1, co...]
    pallas_call x1, Pallas kernels: 2.57 us -> 3.42 us  [dedisperse_own(): pl.pallas_call(own_kernel, out_shape=pltpu.VMEM((LANES * beams, LANES), F...]
  transfers between devices with their start and end apart: 2 -> 2, of which waited for: 2 -> 2; matrix products, arithmetic and copies ran while one was open for 0% -> 0% of each run, Pallas kernels for 8% -> 10%
where the time goes in v4:
time: 45 us; the launch traced here: 44.5 us
  Pallas kernels  19 us (42%)
  starting transfers between devices  14.5 us (32%)
  waiting for transfers between devices  10.7 us (24%)
    all_to_all x1, starting transfers between devices, per_device(): lax.all_to_all(codes, 'chan', split_axis=0, concat_axis=0, tiled=True)  13 us
    pallas_call x1, Pallas kernels, beamform(): pl.pallas_call(functools.partial(beamform_kernel, chunk, width, late), in...  12.1 us
    all_to_all x1, waiting for transfers between devices, per_device(): lax.all_to_all(codes, 'chan', split_axis=0, concat_axis=0, tiled=True)  10.5 us
    pallas_call x1, Pallas kernels, dedisperse_own(): pl.pallas_call(own_kernel, out_shape=pltpu.VMEM((LANES * beams, LANES), F...  3.42 us
    pallas_call x1, Pallas kernels, add_tail(): pl.pallas_call(tail_kernel, out_shape=jax.ShapeDtypeStruct(own.shape, F32...  1.78 us
    ppermute x1, starting transfers between devices, from_behind(): lax.ppermute(value, axis, [(source, source - 1) for source in range(1, co...  1.47 us
    pallas_call x1, Pallas kernels, make_taps(): pl.pallas_call(taps_kernel, out_shape=pltpu.VMEM((LANES, TAPS * LANES), B...  1.23 us
  transfers between devices with their start and end apart: 2, of which 2 were waited for; matrix products, arithmetic and copies ran while one was open for 0% of the time, Pallas kernels for 10%

profile of v4, /device:TPU:1, one launch (start us, length us, event | category | flops | bytes accessed | tf_op | source)
XLA Modules:
  0.0 44.5 jit_solution(7282686354095984686)
XLA Ops:
  0.0 0.0 copy-start
  0.0 0.0 copy-start.1
  0.0 12.1 %shard_map.74 = bf16[64,16,128]{2,1,0:T(8,128)(2,1)} custom-call(bf16[2,2,512,2048]{3,2,1,0:T(8,128)(2,1)} %v_hbm.1, bf16[2,2,512,512]{3,2,1,0:T(8,128)(2,1)} %w_hbm.1), custom_call_target="tpu_custom_call" | custom-call | tf_op jit(solution)/shard_map/pallas_call | solution.py:104
  12.1 13.0 %all-to-all-start = ((bf16[64,16,128]{2,1,0:T(8,128)(2,1)}), bf16[64,16,128]{2,1,0:T(8,128)(2,1)S(1)}, u32[]{:S(2)}, u32[]{:S(2)}) async-start(bf16[64,16,128]{2,1,0:T(8,128)(2,1)} %shard_map.74), calls=%async_computation | async-start | bytes 524288 | tf_op jit(solution)/shard_map/all_to_all | solution.py:280
  25.1 0.0 copy-done
  25.1 0.1 copy.8.baseline_ref
  25.2 0.0 copy-done.1
  25.2 0.1 copy.9.gains_ref
  25.3 1.2 %shard_map.73.taps_ref = bf16[128,4096]{1,0:T(8,128)(2,1)S(1)} custom-call(s32[1,128]{1,0:T(1,128)} %bitcast.2, s32[4,128]{1,0:T(4,128)} %shifts_ref.1, s32[8,8]{1,0:T(8,128)} %delays_ref.1), custom_call_target="tpu_custom_call" | custom-call | flops 4000000 | bytes 1100000 | tf_op jit(solution)/shard_map/pallas_call | solution.py:151
  26.5 10.5 %all-to-all-done.codes_ref = bf16[64,16,128]{2,1,0:T(8,128)(2,1)S(1)} async-done(((bf16[64,16,128]{2,1,0:T(8,128)(2,1)}), bf16[64,16,128]{2,1,0:T(8,128)(2,1)S(1)}, u32[]{:S(2)}, u32[]{:S(2)}) %all-to-all-start) | async-done | bytes 262176 | tf_op jit(solution)/shard_map/all_to_all | solution.py:280
  37.1 0.5 %shard_map.75 = bf16[2,128,128]{2,1,0:T(8,128)(2,1)S(1)} custom-call(bf16[64,16,128]{2,1,0:T(8,128)(2,1)S(1)} %all-to-all-done.codes_ref, f32[128,8]{1,0:T(8,128)S(1)} %copy.8.baseline_ref, f32[128,8]{1,0:T(8,128)S(1)} %copy.9.gains_ref), custom_call_target="tpu_custom_call" | custom-call | flops 1000000 | bytes 400000 | tf_op jit(solution)/shard_map/pallas_call | solution.py:185
  37.6 1.5 %collective-permute-start = (bf16[2,128,128]{2,1,0:T(8,128)(2,1)S(1)}, bf16[2,128,128]{2,1,0:T(8,128)(2,1)S(1)}, u32[]{:S(2)}, u32[]{:S(2)}) collective-permute-start(bf16[2,128,128]{2,1,0:T(8,128)(2,1)S(1)} %shard_map.75), channel_id=1, source_target_pairs={{1,0},{2,1},{3,2},{5,4},{6,5},{7,6},{9,8},{10,9},{11,10},{13,12},{... | collective-permute-start | bytes 196616 | tf_op jit(solution)/shard_map/ppermute | solution.py:274
  39.1 3.4 %shard_map.76.own_ref = f32[1024,128]{1,0:T(8,128)S(1)} custom-call(bf16[128,4096]{1,0:T(8,128)(2,1)S(1)} %shard_map.73.taps_ref, bf16[64,16,128]{2,1,0:T(8,128)(2,1)S(1)} %all-to-all-done.codes_ref, f32[128,8]{1,0:T(8,128)S(1)} %copy.8.baseline_ref, f32[128,8]{1,0:T(8,128)S(1)} %copy.9.gains_ref), custom_call_target="tpu_custom_call" | custom-call | flops 4000000000 | bytes 3000000 | tf_op jit(solution)/shard_map/pallas_call | solution.py:217
  42.5 0.1 collective-permute-done.tail_ref
  42.6 1.8 %shard_map.77 = f32[1024,128]{1,0:T(8,128)} custom-call(bf16[128,4096]{1,0:T(8,128)(2,1)S(1)} %shard_map.73.taps_ref, bf16[2,128,128]{2,1,0:T(8,128)(2,1)S(1)} %collective-permute-done.tail_ref, f32[1024,128]{1,0:T(8,128)S(1)} %shard_map.76.own_ref), custom_call_target="tpu_custom_call" | custom-call | flops 1000000000 | bytes 2000000 | tf_op jit(solution)/shard_map/pallas_call | solution.py:257
Async XLA Ops:
  0.0 25.1 %copy-start = (f32[128,8]{0,1:T(8,128)S(1)}, f32[128,8]{0,1:T(8,128)}, u32[]{:S(2)}) copy-start(f32[128,8]{0,1:T(8,128)} %param.9) | copy-start | bytes 12292
  0.0 25.2 %copy-start.1 = (f32[128,8]{0,1:T(8,128)S(1)}, f32[128,8]{0,1:T(8,128)}, u32[]{:S(2)}) copy-start(f32[128,8]{0,1:T(8,128)} %param.10) | copy-start | bytes 12292
  12.1 25.0 %all-to-all-start = ((bf16[64,16,128]{2,1,0:T(8,128)(2,1)}), bf16[64,16,128]{2,1,0:T(8,128)(2,1)S(1)}, u32[]{:S(2)}, u32[]{:S(2)}) async-start(bf16[64,16,128]{2,1,0:T(8,128)(2,1)} %shard_map.74), calls=%async_computation | async-start | bytes 524288 | tf_op jit(solution)/shard_map/all_to_all | solution.py:280
  37.6 5.0 %collective-permute-start = (bf16[2,128,128]{2,1,0:T(8,128)(2,1)S(1)}, bf16[2,128,128]{2,1,0:T(8,128)(2,1)S(1)}, u32[]{:S(2)}, u32[]{:S(2)}) collective-permute-start(bf16[2,128,128]{2,1,0:T(8,128)(2,1)S(1)} %shard_map.75), channel_id=1, source_target_pairs={{1,0},{2,1},{3,2},{5,4},{6,5},{7,6},{9,8},{10,9},{11,10},{13,12},{... | collective-permute-start | bytes 196616 | tf_op jit(solution)/shard_map/ppermute | solution.py:274

commit v5 on v4

--- a/solution.py
+++ b/solution.py
@@ -119,6 +119,7 @@
 LEVELS = 4
 TREE = 16
 TAPS = 32
+FINE = 8
 VMEM = 24 * 1024 * 1024
 
 
@@ -229,21 +230,32 @@
     groups = tail_ref.shape[0]
     per = LANES // TAPS
     beams = groups * per
-    lane = lax.broadcasted_iota(jnp.int32, (LANES, LANES), 1)
+    lane = lax.broadcasted_iota(jnp.int32, (LANES, LANES), 1) & (TAPS - 1)
     for j in range(groups):
         x = tail_ref[j].astype(F32)
-        for d in range(TAPS):
-            keep = (lane & (TAPS - 1)) >= TAPS - d
-            moved = jnp.where(keep, pltpu.roll(x, (TAPS - d) % LANES, 1), 0.0)
-            window[d * LANES : (d + 1) * LANES, j * LANES : (j + 1) * LANES] = moved.astype(BF16)
-    added = jnp.dot(taps_ref[...], window[...], preferred_element_type=F32)
+        for e in range(FINE):
+            moved = jnp.where(lane >= FINE - e, pltpu.roll(x, FINE - e, 1), 0.0)
+            window[e * LANES : (e + 1) * LANES, j * LANES : (j + 1) * LANES] = moved.astype(BF16)
+    depth = FINE * LANES
+    coarse = jnp.concatenate([taps_ref[:, a * depth : (a + 1) * depth] for a in range(TAPS // FINE)], axis=0)
+    sums = jnp.dot(coarse, window[...], preferred_element_type=F32)
+    added = []
+    for j in range(groups):
+        whole = None
+        for a in range(TAPS // FINE):
+            y = sums[a * LANES : (a + 1) * LANES, j * LANES : (j + 1) * LANES]
+            steps = TAPS - FINE - a * FINE
+            if steps:
+                y = jnp.where(lane >= steps, pltpu.roll(y, steps, 1), 0.0)
+            whole = y if whole is None else whole + y
+        added.append(whole)
     last = lax.broadcasted_iota(jnp.int32, (TREE, LANES), 1) >= LANES - TAPS
     copies = []
     for q in range(LANES // TREE):
         for b in range(beams):
             rows = pl.ds(q * TREE * beams + b, TREE, stride=beams)
             j, i = divmod(b, per)
-            piece = added[q * TREE : (q + 1) * TREE, j * LANES : (j + 1) * LANES]
+            piece = added[j][q * TREE : (q + 1) * TREE, :]
             piece = pltpu.roll(piece, (per - 1 - i) * TAPS, 1)
             total[rows, :] = own_ref[rows, :] + jnp.where(last, piece, 0.0)
         block = pl.ds(q * TREE * beams, TREE * beams)
@@ -260,7 +272,7 @@
         in_specs=[pl.BlockSpec(memory_space=pltpu.VMEM)] * 3,
         out_specs=pl.BlockSpec(memory_space=pl.ANY),
         scratch_shapes=[
-            pltpu.VMEM((TAPS * LANES, 2 * LANES), BF16),
+            pltpu.VMEM((FINE * LANES, 2 * LANES), BF16),
             pltpu.VMEM(own.shape, F32),
             pltpu.SemaphoreType.DMA((LANES // TREE,)),
         ],

time: 45 us -> 44.7 us (level)
  no operation moved by 1% of the time
where the time goes in v5:
time: 44.7 us; the launch traced here: 44.3 us
  Pallas kernels  18.7 us (42%)
  starting transfers between devices  14.5 us (32%)
  waiting for transfers between devices  10.7 us (24%)
    all_to_all x1, starting transfers between devices, per_device(): lax.all_to_all(codes, 'chan', split_axis=0, concat_axis=0, tiled=True)  13 us
    pallas_call x1, Pallas kernels, beamform(): pl.pallas_call(functools.partial(beamform_kernel, chunk, width, late), in...  12.1 us
    all_to_all x1, waiting for transfers between devices, per_device(): lax.all_to_all(codes, 'chan', split_axis=0, concat_axis=0, tiled=True)  10.5 us
    pallas_call x1, Pallas kernels, dedisperse_own(): pl.pallas_call(own_kernel, out_shape=pltpu.VMEM((LANES * beams, LANES), F...  3.42 us
    pallas_call x1, Pallas kernels, add_tail(): pl.pallas_call(tail_kernel, out_shape=jax.ShapeDtypeStruct(own.shape, F32...  1.53 us
    ppermute x1, starting transfers between devices, from_behind(): lax.ppermute(value, axis, [(source, source - 1) for source in range(1, co...  1.47 us
    pallas_call x1, Pallas kernels, make_taps(): pl.pallas_call(taps_kernel, out_shape=pltpu.VMEM((LANES, TAPS * LANES), B...  1.23 us
  transfers between devices with their start and end apart: 2, of which 2 were waited for; matrix products, arithmetic and copies ran while one was open for 0% of the time, Pallas kernels for 10%

profile of v5, /device:TPU:1, one launch (start us, length us, event | category | flops | bytes accessed | tf_op | source)
XLA Modules:
  0.0 44.3 jit_solution(446130944150616059)
XLA Ops:
  0.0 0.0 copy-start
  0.0 0.0 copy-start.1
  0.0 12.1 %shard_map.74 = bf16[64,16,128]{2,1,0:T(8,128)(2,1)} custom-call(bf16[2,2,512,2048]{3,2,1,0:T(8,128)(2,1)} %v_hbm.1, bf16[2,2,512,512]{3,2,1,0:T(8,128)(2,1)} %w_hbm.1), custom_call_target="tpu_custom_call" | custom-call | tf_op jit(solution)/shard_map/pallas_call | solution.py:104
  12.1 13.0 %all-to-all-start = ((bf16[64,16,128]{2,1,0:T(8,128)(2,1)}), bf16[64,16,128]{2,1,0:T(8,128)(2,1)S(1)}, u32[]{:S(2)}, u32[]{:S(2)}) async-start(bf16[64,16,128]{2,1,0:T(8,128)(2,1)} %shard_map.74), calls=%async_computation | async-start | bytes 524288 | tf_op jit(solution)/shard_map/all_to_all | solution.py:292
  25.1 0.0 copy-done
  25.1 0.1 copy.8.baseline_ref
  25.2 0.0 copy-done.1
  25.2 0.1 copy.9.gains_ref
  25.3 1.2 %shard_map.73.taps_ref = bf16[128,4096]{1,0:T(8,128)(2,1)S(1)} custom-call(s32[1,128]{1,0:T(1,128)} %bitcast.2, s32[4,128]{1,0:T(4,128)} %shifts_ref.1, s32[8,8]{1,0:T(8,128)} %delays_ref.1), custom_call_target="tpu_custom_call" | custom-call | flops 4000000 | bytes 1100000 | tf_op jit(solution)/shard_map/pallas_call | solution.py:152
  26.5 10.5 %all-to-all-done.codes_ref = bf16[64,16,128]{2,1,0:T(8,128)(2,1)S(1)} async-done(((bf16[64,16,128]{2,1,0:T(8,128)(2,1)}), bf16[64,16,128]{2,1,0:T(8,128)(2,1)S(1)}, u32[]{:S(2)}, u32[]{:S(2)}) %all-to-all-start) | async-done | bytes 262176 | tf_op jit(solution)/shard_map/all_to_all | solution.py:292
  37.1 0.5 %shard_map.75 = bf16[2,128,128]{2,1,0:T(8,128)(2,1)S(1)} custom-call(bf16[64,16,128]{2,1,0:T(8,128)(2,1)S(1)} %all-to-all-done.codes_ref, f32[128,8]{1,0:T(8,128)S(1)} %copy.8.baseline_ref, f32[128,8]{1,0:T(8,128)S(1)} %copy.9.gains_ref), custom_call_target="tpu_custom_call" | custom-call | flops 1000000 | bytes 400000 | tf_op jit(solution)/shard_map/pallas_call | solution.py:186
  37.6 1.5 %collective-permute-start = (bf16[2,128,128]{2,1,0:T(8,128)(2,1)S(1)}, bf16[2,128,128]{2,1,0:T(8,128)(2,1)S(1)}, u32[]{:S(2)}, u32[]{:S(2)}) collective-permute-start(bf16[2,128,128]{2,1,0:T(8,128)(2,1)S(1)} %shard_map.75), channel_id=1, source_target_pairs={{1,0},{2,1},{3,2},{5,4},{6,5},{7,6},{9,8},{10,9},{11,10},{13,12},{... | collective-permute-start | bytes 196616 | tf_op jit(solution)/shard_map/ppermute | solution.py:286
  39.1 3.4 %shard_map.76.own_ref = f32[1024,128]{1,0:T(8,128)S(1)} custom-call(bf16[128,4096]{1,0:T(8,128)(2,1)S(1)} %shard_map.73.taps_ref, bf16[64,16,128]{2,1,0:T(8,128)(2,1)S(1)} %all-to-all-done.codes_ref, f32[128,8]{1,0:T(8,128)S(1)} %copy.8.baseline_ref, f32[128,8]{1,0:T(8,128)S(1)} %copy.9.gains_ref), custom_call_target="tpu_custom_call" | custom-call | flops 4000000000 | bytes 3000000 | tf_op jit(solution)/shard_map/pallas_call | solution.py:218
  42.5 0.1 collective-permute-done.tail_ref
  42.6 1.5 %shard_map.77 = f32[1024,128]{1,0:T(8,128)} custom-call(bf16[128,4096]{1,0:T(8,128)(2,1)S(1)} %shard_map.73.taps_ref, bf16[2,128,128]{2,1,0:T(8,128)(2,1)S(1)} %collective-permute-done.tail_ref, f32[1024,128]{1,0:T(8,128)S(1)} %shard_map.76.own_ref), custom_call_target="tpu_custom_call" | custom-call | flops 1000000000 | bytes 2000000 | tf_op jit(solution)/shard_map/pallas_call | solution.py:269
Async XLA Ops:
  0.0 25.1 %copy-start = (f32[128,8]{0,1:T(8,128)S(1)}, f32[128,8]{0,1:T(8,128)}, u32[]{:S(2)}) copy-start(f32[128,8]{0,1:T(8,128)} %param.9) | copy-start | bytes 12292
  0.0 25.2 %copy-start.1 = (f32[128,8]{0,1:T(8,128)S(1)}, f32[128,8]{0,1:T(8,128)}, u32[]{:S(2)}) copy-start(f32[128,8]{0,1:T(8,128)} %param.10) | copy-start | bytes 12292
  12.1 25.0 %all-to-all-start = ((bf16[64,16,128]{2,1,0:T(8,128)(2,1)}), bf16[64,16,128]{2,1,0:T(8,128)(2,1)S(1)}, u32[]{:S(2)}, u32[]{:S(2)}) async-start(bf16[64,16,128]{2,1,0:T(8,128)(2,1)} %shard_map.74), calls=%async_computation | async-start | bytes 524288 | tf_op jit(solution)/shard_map/all_to_all | solution.py:292
  37.6 5.0 %collective-permute-start = (bf16[2,128,128]{2,1,0:T(8,128)(2,1)S(1)}, bf16[2,128,128]{2,1,0:T(8,128)(2,1)S(1)}, u32[]{:S(2)}, u32[]{:S(2)}) collective-permute-start(bf16[2,128,128]{2,1,0:T(8,128)(2,1)S(1)} %shard_map.75), channel_id=1, source_target_pairs={{1,0},{2,1},{3,2},{5,4},{6,5},{7,6},{9,8},{10,9},{11,10},{13,12},{... | collective-permute-start | bytes 196616 | tf_op jit(solution)/shard_map/ppermute | solution.py:286
